TPU v7x, 512 devices: a whole 4x8x8 slice. The times are simulated.
512 devices in a mesh: replica: 32 (over y_lo, z), fsdp: 16 (over x, y_hi, core).
Axes of the slice: x: 4, y: 8 (y_hi: 2, y_lo: 4; y = y_hi * 4 + y_lo), z: 8, core: 2. Of those that a mesh axis runs over, the one named last changes fastest.
Arguments:
- activations: bfloat16 [131072, 4608], P(('replica', 'fsdp')), may hold values from -6 to 6
- base_master: float32 [4608, 1024], P(('fsdp', 'replica')), may hold values from -6 to 6
- momentum: float32 [4608, 1024], P(('fsdp', 'replica')), may hold values from -4 to 4
- inner_weights: bfloat16 [32, 4608, 1024], P('replica', 'fsdp'), may hold values from -6 to 6
Outputs:
- keys: bfloat16 [131072, 1024], P(('replica', 'fsdp'))
- base_out: float32 [4608, 1024], P(('fsdp', 'replica'))
- momentum_out: float32 [4608, 1024], P(('fsdp', 'replica'))
All inputs are finite; a program needn't handle non-finite values.
Results may differ from a plain program's by a relative error of at most 0.024.
Values may be sent and summed in bfloat16 or wider, within the bound.
No kernel may reach another device: no remote copies, remote signals or barrier semaphores. Data moves between devices by JAX's collectives and lax.ppermute only.
A program may use at most 64 MiB of HBM per device.

v0:
```python
import jax
import jax.numpy as jnp
from jax import lax
from jax.sharding import PartitionSpec as P

D = 4608
BLK = 128


def encode(delta):
    blocks = delta.reshape(delta.shape[0], delta.shape[1] // BLK, BLK)
    largest = jnp.max(jnp.abs(blocks), axis=-1, keepdims=True)
    scales = (largest + 1e-06) / 448.0
    coded = (blocks / scales).astype(jnp.bfloat16)
    return (coded, scales)


def body(activations, base_master, momentum, inner_weights):
    replicas = lax.axis_size("replica")
    owned = base_master.shape[0]
    width = base_master.shape[1]
    nblocks = width // BLK
    shard_base = lax.all_gather(
        base_master.astype(jnp.bfloat16), "replica", axis=0, tiled=True
    ).astype(base_master.dtype)
    delta = shard_base - inner_weights[0].astype(jnp.float32)
    coded, scales = encode(delta)
    coded = coded.reshape(replicas, owned, width)
    scales = scales.reshape(replicas, owned, nblocks)
    got_coded, got_scales = (
        lax.all_to_all(coded, "replica", split_axis=0, concat_axis=0, tiled=True),
        lax.all_to_all(
            scales.astype(jnp.bfloat16), "replica", split_axis=0, concat_axis=0, tiled=True
        ).astype(scales.dtype),
    )
    decoded = (
        got_coded.reshape(replicas, owned, nblocks, BLK).astype(jnp.float32) * got_scales[..., None]
    )
    outer_grad = jnp.sum(decoded, axis=0).reshape(owned, width) / replicas
    momentum_out = 0.9 * momentum + outer_grad
    base_out = base_master - 0.7 * (outer_grad + 0.9 * momentum_out)
    fragment = base_out.astype(jnp.bfloat16)
    shard_rows = lax.all_gather(fragment, "replica", axis=0, tiled=True)
    total = jnp.dot(
        activations,
        lax.all_gather(shard_rows, "fsdp", axis=0, tiled=True),
        preferred_element_type=jnp.float32,
    )
    keys = (total * D ** (-0.5)).astype(jnp.bfloat16)
    return (keys, base_out, momentum_out)


def solution(mesh):
    return jax.shard_map(
        body,
        mesh=mesh,
        in_specs=(
            P(("replica", "fsdp"), None),
            P(("fsdp", "replica"), None),
            P(("fsdp", "replica"), None),
            P("replica", "fsdp", None),
        ),
        out_specs=(
            P(("replica", "fsdp"), None),
            P(("fsdp", "replica"), None),
            P(("fsdp", "replica"), None),
        ),
        check_vma=False,
    )
```

profile of v0, /device:TPU:1, one launch (start us, length us, event | category | flops | bytes accessed | tf_op | source)
XLA Modules:
  0.0 367.1 jit_solution(17252448288701154971)
XLA Ops:
  7.2 0.0 copy-start
  7.2 1.0 convert_bitcast_fusion.1
  8.2 82.0 %all-gather = bf16[32,9,1024]{2,1,0:T(8,128)(2,1)} all-gather(bf16[1,9,1024]{2,1,0:T(8,128)(2,1)S(1)} %convert_bitcast_fusion.1), channel_id=1, replica_groups=mesh['replica'=32,'fsdp'=16] {'replica'}, dimensions={0}, use_global_device_ids=true | all-gather | bytes 608256 | tf_op jit(solution)/shard_map/all_gather | solution.py:23
  90.1 1.4 reshape.40
  91.6 2.3 abs_bitcast_fusion
  93.8 0.2 copy.24
  94.1 1.0 reduce_max.9
  95.1 1.0 copy.17
  96.1 0.2 convert_element_type.45
  96.3 0.7 copy.19
  97.0 4.6 %all-to-all-start.1 = ((bf16[32,9,8]{1,2,0:T(8,128)(2,1)}), bf16[32,9,8]{1,2,0:T(8,128)(2,1)}, u32[]{:S(2)}, u32[]{:S(2)}) async-start(bf16[32,9,8]{1,2,0:T(8,128)(2,1)} %copy.19), calls=%async_computation.1 | async-start | bytes 131072 | tf_op jit(solution)/shard_map/all_to_all | solution.py:32
  101.5 0.8 copy.18
  102.3 1.3 div.25
  103.6 1.5 div.26
  105.1 2.7 reshape.34
  107.8 3.6 divide_convert_fusion
  111.4 0.0 all-to-all-done.1
  111.4 9.6 %all-to-all-start = ((bf16[32,9,1024]{2,1,0:T(8,128)(2,1)}), bf16[32,9,1024]{2,1,0:T(8,128)(2,1)}, u32[]{:S(2)}, u32[]{:S(2)}) async-start(bf16[32,9,1024]{2,1,0:T(8,128)(2,1)} %divide_convert_fusion), calls=%async_computation | async-start | bytes 2097152 | tf_op jit(solution)/shard_map/all_to_all | solution.py:31
  121.0 0.0 all-gather.4.cloned.1.call-start
  121.1 1.0 copy.20
  122.0 0.1 copy.21
  122.1 1.4 mul.30
  123.5 1.5 mul.31
  125.0 12.5 %all-to-all-done = bf16[32,9,1024]{2,1,0:T(8,128)(2,1)} async-done(((bf16[32,9,1024]{2,1,0:T(8,128)(2,1)}), bf16[32,9,1024]{2,1,0:T(8,128)(2,1)}, u32[]{:S(2)}, u32[]{:S(2)}) %all-to-all-start) | async-done | bytes 589856 | tf_op jit(solution)/shard_map/all_to_all | solution.py:31
  137.5 2.0 fusion
  139.5 0.7 convert_bitcast_fusion
  140.2 73.8 %all-gather.1 = bf16[32,9,1024]{2,1,0:T(8,128)(2,1)S(1)} all-gather(bf16[1,9,1024]{2,1,0:T(8,128)(2,1)S(1)} %get-tuple-element.15), channel_id=1, replica_groups=mesh['replica'=32,'fsdp'=16] {'replica'}, dimensions={0}, use_global_device_ids=true | all-gather | bytes 608256 | tf_op jit(solution)/shard_map/all_gather | solution.py:43
  214.0 1.1 reshape.39
  215.1 0.0 all-gather.4.cloned.1.call-update
  215.1 137.8 %all-gather.4.cloned.1.call-done = bf16[4608,1024]{1,0:T(8,128)(2,1)} async-done(((bf16[288,1024]{1,0:T(8,128)(2,1)}), bf16[4608,1024]{1,0:T(8,128)(2,1)}) %all-gather.4.cloned.1.call-update) | async-done | bytes 9437200 | tf_op jit(solution)/shard_map/all_gather | solution.py:46
  352.9 6.3 %fusion.2 = bf16[256,1024]{0,1:T(8,128)(2,1)S(1)} fusion(bf16[4608,1024]{1,0:T(8,128)(2,1)} %all-gather.4.cloned.1.call-done, bf16[256,4608]{1,0:T(8,128)(2,1)S(1)} %copy-done), kind=kOutput, calls=%fused_computation.5 | convolution fusion | flops 2416443392 | bytes 12320768 | tf_op jit(solution)/shard_map/dot_general | solution.py:44
  359.2 1.0 copy.23
  (6 shorter events, 0.0 us)
Async XLA Ops:
  7.2 345.7 %copy-start = (bf16[256,4608]{1,0:T(8,128)(2,1)S(1)}, bf16[256,4608]{1,0:T(8,128)(2,1)}, u32[]{:S(2)}) copy-start(bf16[256,4608]{1,0:T(8,128)(2,1)} %param.4) | copy-start | bytes 7077892
  97.0 14.4 %all-to-all-start.1 = ((bf16[32,9,8]{1,2,0:T(8,128)(2,1)}), bf16[32,9,8]{1,2,0:T(8,128)(2,1)}, u32[]{:S(2)}, u32[]{:S(2)}) async-start(bf16[32,9,8]{1,2,0:T(8,128)(2,1)} %copy.19), calls=%async_computation.1 | async-start | bytes 131072 | tf_op jit(solution)/shard_map/all_to_all | solution.py:32
  111.4 26.1 %all-to-all-start = ((bf16[32,9,1024]{2,1,0:T(8,128)(2,1)}), bf16[32,9,1024]{2,1,0:T(8,128)(2,1)}, u32[]{:S(2)}, u32[]{:S(2)}) async-start(bf16[32,9,1024]{2,1,0:T(8,128)(2,1)} %divide_convert_fusion), calls=%async_computation | async-start | bytes 2097152 | tf_op jit(solution)/shard_map/all_to_all | solution.py:31
  121.0 231.9 %all-gather.4.cloned.1.call-start = ((), (), s32[]{:S(2)}) async-start(), calls=%async_computation.2 | async-start | bytes 10027008 | tf_op jit(solution)/shard_map/all_gather | solution.py:46
  137.5 2.0 copy-start.1
  137.5 2.0 copy-start.2
Sparse Core Ops, SparseCore 0:
  215.2 137.6 all-gather.3
where the time goes:
time: 369 us; the launch traced here: 367 us
  blocking collectives  156 us (42%)
  waiting for transfers between devices  150 us (41%)
  local copies, waits for them, and re-layouts  15.7 us (4%)
  starting transfers between devices  14.2 us (4%)
  between operations  14.1 us (4%)
  other arithmetic  10.6 us (3%)
  matrix products  6.33 us (2%)
    all_gather x1, waiting for transfers between devices, body(): lax.all_gather(shard_rows, 'fsdp', axis=0, tiled=True)  138 us
    all_gather x1, blocking collectives, body(): lax.all_gather(base_master.astype(jnp.bfloat16), 'replica', axis=0, tiled...  82 us
    all_gather x1, blocking collectives, body(): shard_rows = lax.all_gather(fragment, 'replica', axis=0, tiled=True)  73.8 us
    all_to_all x1, waiting for transfers between devices, body(): lax.all_to_all(coded, 'replica', split_axis=0, concat_axis=0, tiled=True)  12.5 us
    all_to_all x1, starting transfers between devices, body(): lax.all_to_all(coded, 'replica', split_axis=0, concat_axis=0, tiled=True)  9.63 us
  transfers between devices with their start and end apart: 3, of which 2 were waited for; matrix products, arithmetic and copies ran while one was open for 4% of the time, Pallas kernels for 0%

commit v1 on v0

v1 whole, which is shorter than its diff:
```python
import jax
import jax.numpy as jnp
from jax import lax
from jax.experimental import pallas as pl
from jax.experimental.pallas import tpu as pltpu
from jax.sharding import Mesh, PartitionSpec as P

D = 4608
BLK = 128
AXES = ("yl", "z", "x", "yh", "c")
SIZES = (4, 8, 4, 2, 2)
REPLICAS = 32
ROWS = ("yh", "yl", "z")


def outer_kernel(inner_ref, base_ref, mom_ref, base_out_ref, mom_out_ref, frag_ref):
    base = base_ref[...]
    total = jnp.zeros_like(base)
    for r in range(REPLICAS):
        delta = base - inner_ref[r].astype(jnp.float32)
        largest = jnp.max(jnp.abs(delta), axis=-1, keepdims=True)
        scales = (largest + 1e-06) / 448.0
        coded = (delta / scales).astype(jnp.bfloat16)
        total = total + coded.astype(jnp.float32) * scales
    outer_grad = total / REPLICAS
    momentum_out = 0.9 * mom_ref[...] + outer_grad
    base_out = base - 0.7 * (outer_grad + 0.9 * momentum_out)
    mom_out_ref[...] = momentum_out
    base_out_ref[...] = base_out
    frag_ref[...] = base_out.astype(jnp.bfloat16)


def outer_step(got, base, mom):
    n = base.shape[0]
    f32 = jax.ShapeDtypeStruct((n, BLK), jnp.float32)
    return pl.pallas_call(
        outer_kernel,
        out_shape=(f32, f32, jax.ShapeDtypeStruct((n, BLK), jnp.bfloat16)),
        name="outer_step",
    )(got, base, mom)


def shift(v, axis, by):
    n = lax.axis_size(axis)
    return lax.ppermute(v, axis, [(i, (i + by) % n) for i in range(n)])


def body(activations, base_master, momentum, inner_weights):
    owned, width = base_master.shape
    nx = lax.axis_size("x")
    x = lax.axis_index("x")
    c = lax.axis_index("c")
    flat = owned * width // BLK
    depth = activations.shape[1] // nx

    got = lax.all_to_all(
        inner_weights.reshape(REPLICAS, flat, BLK), ("yl", "z"), split_axis=0, concat_axis=0, tiled=True
    )

    def columns(by):
        return lax.dynamic_slice_in_dim(activations, lax.rem(x + (by + nx), nx) * depth, depth, axis=1)

    acts = {by: shift(columns(by), "x", by) for by in (2, 1, -1)}
    got, acts[1], acts[-1] = lax.optimization_barrier((got, acts[1], acts[-1]))

    base_flat, mom_flat, frag = outer_step(
        got, base_master.reshape(flat, BLK), momentum.reshape(flat, BLK)
    )
    pieces = 64
    mine = lax.all_to_all(
        jnp.broadcast_to(frag[None], (pieces, flat, BLK)), ROWS, split_axis=0, concat_axis=0, tiled=True
    )
    mine, acts[2] = lax.optimization_barrier((mine, acts[2]))
    mine = mine.reshape(2, REPLICAS * owned, width)
    other = shift(mine, "c", 1)
    first = jnp.where(c == 0, mine, other)
    second = jnp.where(c == 0, other, mine)
    rows = jnp.stack([first, second], axis=1).reshape(depth, width)

    total = jnp.dot(columns(0), rows, preferred_element_type=jnp.float32)
    for by in (2, 1, -1):
        part = jnp.dot(acts[by], rows, preferred_element_type=jnp.float32).astype(jnp.bfloat16)
        total = total + shift(part, "x", -by).astype(jnp.float32)
    keys = (total * D ** (-0.5)).astype(jnp.bfloat16)
    return keys, base_flat.reshape(owned, width), mom_flat.reshape(owned, width)


def solution(mesh):
    fine = Mesh(mesh.devices.reshape(SIZES), AXES)
    tokens = P(AXES, None)
    owned = P(("x", "yh", "c", "yl", "z"), None)
    return jax.shard_map(
        body,
        mesh=fine,
        in_specs=(tokens, owned, owned, P(("yl", "z"), ("x", "yh", "c"), None)),
        out_specs=(tokens, owned, owned),
        check_vma=False,
    )
```

time: 369 us -> 125 us (0.34)
  blocking collectives: 156 us -> 0 us
  waiting for transfers between devices: 150 us -> 48.1 us
  starting transfers between devices: 14.2 us -> 51.5 us
  between operations: 14.1 us -> 0.85 us
  other arithmetic: 10.6 us -> 2.57 us
  local copies, waits for them, and re-layouts: 15.7 us -> 11.8 us
    all_gather x2 -> x0, blocking collectives: 156 us -> none  [the longest x1 82 us: body(): lax.all_gather(base_master.astype(jnp.bfloat16), 'replica', axis=0, tiled...]
    all_gather x1 -> x0, waiting for transfers between devices: 138 us -> none  [body(): lax.all_gather(shard_rows, 'fsdp', axis=0, tiled=True)]
    ppermute x0 -> x7, waiting for transfers between devices: none -> 35.1 us  [shift(): return lax.ppermute(v, axis, [(i, (i + by) % n) for i in range(n)])]
    ppermute x0 -> x7, starting transfers between devices: none -> 27.3 us  [shift(): return lax.ppermute(v, axis, [(i, (i + by) % n) for i in range(n)])]
    all_to_all x2, starting transfers between devices: 14.2 us -> 24.2 us  [the longest x1 14.3 us: body(): lax.all_to_all(inner_weights.reshape(REPLICAS, flat, BLK), ('yl', 'z'), s...]
    reshape x1 -> x6, local copies, waits for them, and re-layouts: 2.66 us -> 7.01 us  [the longest x1 2.26 us: body(): inner_weights.reshape(REPLICAS, flat, BLK)]
    unnamed x3 -> x0, other arithmetic: 3.95 us -> none
  transfers between devices with their start and end apart: 3 -> 9, of which waited for: 2 -> 7; matrix products, arithmetic and copies ran while one was open for 4% -> 9% of each run, Pallas kernels for 0% -> 0%
where the time goes in v1:
time: 125 us; the launch traced here: 124 us
  starting transfers between devices  51.5 us (41%)
  waiting for transfers between devices  48.1 us (38%)
  local copies, waits for them, and re-layouts  11.8 us (9%)
  matrix products  6.86 us (5%)
  other arithmetic  2.57 us (2%)
  Pallas kernels  2.17 us (2%)
    ppermute x7, waiting for transfers between devices, shift(): return lax.ppermute(v, axis, [(i, (i + by) % n) for i in range(n)])  35.1 us
    ppermute x7, starting transfers between devices, shift(): return lax.ppermute(v, axis, [(i, (i + by) % n) for i in range(n)])  27.3 us
    all_to_all x1, starting transfers between devices, body(): lax.all_to_all(inner_weights.reshape(REPLICAS, flat, BLK), ('yl', 'z'), s...  14.3 us
    all_to_all x1, waiting for transfers between devices, body(): lax.all_to_all(jnp.broadcast_to(frag[None], (pieces, flat, BLK)), ROWS, s...  13.1 us
    all_to_all x1, starting transfers between devices, body(): lax.all_to_all(jnp.broadcast_to(frag[None], (pieces, flat, BLK)), ROWS, s...  9.91 us
    dot_general x3, matrix products, body(): jnp.dot(acts[by], rows, preferred_element_type=jnp.float32)  4.96 us
  transfers between devices with their start and end apart: 9, of which 7 were waited for; matrix products, arithmetic and copies ran while one was open for 9% of the time, Pallas kernels for 0%

profile of v1, /device:TPU:1, one launch (start us, length us, event | category | flops | bytes accessed | tf_op | source)
XLA Modules:
  0.0 123.9 jit_solution(1506758258134667330)
XLA Ops:
  0.6 2.3 %reshape.28 = bf16[32,72,128]{2,1,0:T(8,128)(2,1)} reshape(bf16[1,288,1024]{2,1,0:T(8,128)(2,1)} %param.7) | data formatting | bytes 1179648 | tf_op jit(solution)/shard_map/reshape | solution.py:57
  2.9 14.3 %all-to-all-start = ((bf16[32,72,128]{2,1,0:T(8,128)(2,1)}), bf16[32,72,128]{2,1,0:T(8,128)(2,1)S(1)}, u32[]{:S(2)}, u32[]{:S(2)}) async-start(bf16[32,72,128]{2,1,0:T(8,128)(2,1)} %reshape.28), calls=%async_computation | async-start | bytes 1179648 | tf_op jit(solution)/shard_map/all_to_all | solution.py:56
  17.2 1.2 constant_dynamic-slice_fusion
  18.4 3.1 %collective-permute-start = (bf16[256,1152]{1,0:T(8,128)(2,1)}, bf16[256,1152]{1,0:T(8,128)(2,1)S(1)}, u32[]{:S(2)}, u32[]{:S(2)}) collective-permute-start(bf16[256,1152]{1,0:T(8,128)(2,1)} %get-tuple-element.22), channel_id=1, source_target_pairs={{0,4},{4,8},{8,12},{12,0},{1,5},{5,9},{9,13},{13,1},{2,6},{6,10},{... | collective-permute-start | bytes 1769480 | tf_op jit(solution)/shard_map/ppermute | solution.py:45
  21.5 3.4 %collective-permute-start.1 = (bf16[256,1152]{1,0:T(8,128)(2,1)}, bf16[256,1152]{1,0:T(8,128)(2,1)S(1)}, u32[]{:S(2)}, u32[]{:S(2)}) collective-permute-start(bf16[256,1152]{1,0:T(8,128)(2,1)} %get-tuple-element.23), channel_id=1, source_target_pairs={{0,12},{4,0},{8,4},{12,8},{1,13},{5,1},{9,5},{13,9},{2,14},{6,2},{... | collective-permute-start | bytes 1769480 | tf_op jit(solution)/shard_map/ppermute | solution.py:45
  24.9 1.5 %reshape.29.base_ref = f32[72,128]{1,0:T(8,128)} reshape(f32[9,1024]{1,0:T(8,128)} %param.5) | data formatting | bytes 73728 | tf_op jit(solution)/shard_map/reshape | solution.py:67
  26.4 1.5 %reshape.30.mom_ref = f32[72,128]{1,0:T(8,128)} reshape(f32[9,1024]{1,0:T(8,128)} %param.6) | data formatting | bytes 73728 | tf_op jit(solution)/shard_map/reshape | solution.py:67
  27.9 7.7 %collective-permute-done = bf16[256,1152]{1,0:T(8,128)(2,1)S(1)} collective-permute-done((bf16[256,1152]{1,0:T(8,128)(2,1)}, bf16[256,1152]{1,0:T(8,128)(2,1)S(1)}, u32[]{:S(2)}, u32[]{:S(2)}) %collective-permute-start) | collective-permute-done | bytes 589856 | tf_op jit(solution)/shard_map/ppermute | solution.py:45
  35.6 1.6 %collective-permute-done.1 = bf16[256,1152]{1,0:T(8,128)(2,1)S(1)} collective-permute-done((bf16[256,1152]{1,0:T(8,128)(2,1)}, bf16[256,1152]{1,0:T(8,128)(2,1)S(1)}, u32[]{:S(2)}, u32[]{:S(2)}) %collective-permute-start.1) | collective-permute-done | bytes 589856 | tf_op jit(solution)/shard_map/ppermute | solution.py:45
  37.2 0.9 copy-done
  38.1 2.2 %outer_step.1 = (f32[72,128]{1,0:T(8,128)}, f32[72,128]{1,0:T(8,128)}, bf16[72,128]{1,0:T(8,128)(2,1)}) custom-call(bf16[32,72,128]{2,1,0:T(8,128)(2,1)} %copy-done, f32[72,128]{1,0:T(8,128)} %reshape.29.base_ref, f32[72,128]{1,0:T(8,128)} %reshape.30.mom_ref), custom_call_target="tpu_custom_call" | custom-call | tf_op jit(solution)/shard_map/outer_step/pallas_call | solution.py:36
  40.3 1.9 %broadcast_in_dim.2 = bf16[64,72,128]{2,1,0:T(8,128)(2,1)} broadcast(bf16[72,128]{1,0:T(8,128)(2,1)} %get-tuple-element.12), dimensions={1,2} | broadcast | bytes 1198080 | tf_op jit(solution)/shard_map/broadcast_in_dim | solution.py:71
  42.2 9.9 %all-to-all-start.1 = ((bf16[64,72,128]{2,1,0:T(8,128)(2,1)}), bf16[64,72,128]{2,1,0:T(8,128)(2,1)S(1)}, u32[]{:S(2)}, u32[]{:S(2)}) async-start(bf16[64,72,128]{2,1,0:T(8,128)(2,1)} %broadcast_in_dim.2), calls=%async_computation.1 | async-start | bytes 2359296 | tf_op jit(solution)/shard_map/all_to_all | solution.py:70
  52.1 4.4 %collective-permute-start.2 = (bf16[256,1152]{1,0:T(8,128)(2,1)S(1)}, bf16[256,1152]{1,0:T(8,128)(2,1)S(1)}, u32[]{:S(2)}, u32[]{:S(2)}) collective-permute-start(bf16[256,1152]{1,0:T(8,128)(2,1)S(1)} %get-tuple-element.21), channel_id=1, source_target_pairs={{0,8},{4,12},{8,0},{12,4},{1,9},{5,13},{9,1},{13,5},{2,10},{6,14},... | collective-permute-start | bytes 1769480 | tf_op jit(solution)/shard_map/ppermute | solution.py:45
  56.5 11.1 %collective-permute-done.2 = bf16[256,1152]{1,0:T(8,128)(2,1)S(1)} collective-permute-done((bf16[256,1152]{1,0:T(8,128)(2,1)S(1)}, bf16[256,1152]{1,0:T(8,128)(2,1)S(1)}, u32[]{:S(2)}, u32[]{:S(2)}) %collective-permute-start.2) | collective-permute-done | bytes 589856 | tf_op jit(solution)/shard_map/ppermute | solution.py:45
  67.6 13.1 %all-to-all-done.1 = bf16[64,72,128]{2,1,0:T(8,128)(2,1)S(1)} async-done(((bf16[64,72,128]{2,1,0:T(8,128)(2,1)}), bf16[64,72,128]{2,1,0:T(8,128)(2,1)S(1)}, u32[]{:S(2)}, u32[]{:S(2)}) %all-to-all-start.1) | async-done | bytes 1179680 | tf_op jit(solution)/shard_map/all_to_all | solution.py:70
  80.7 0.5 reshape.31
  81.2 6.6 %collective-permute-start.3 = (bf16[2,288,1024]{2,1,0:T(8,128)(2,1)S(1)}, bf16[2,288,1024]{2,1,0:T(8,128)(2,1)S(1)}, u32[]{:S(2)}, u32[]{:S(2)}) collective-permute-start(bf16[2,288,1024]{2,1,0:T(8,128)(2,1)S(1)} %reshape.31), channel_id=1, source_target_pairs={{0,1},{1,0},{2,3},{3,2},{4,5},{5,4},{6,7},{7,6},{8,9},{9,8},{10,11... | collective-permute-start | bytes 3538952 | tf_op jit(solution)/shard_map/ppermute | solution.py:45
  87.8 2.4 %collective-permute-done.3 = bf16[2,288,1024]{2,1,0:T(8,128)(2,1)S(1)} collective-permute-done((bf16[2,288,1024]{2,1,0:T(8,128)(2,1)S(1)}, bf16[2,288,1024]{2,1,0:T(8,128)(2,1)S(1)}, u32[]{:S(2)}, u32[]{:S(2)}) %collective-permute-start.3) | collective-permute-done | bytes 1179680 | tf_op jit(solution)/shard_map/ppermute | solution.py:45
  90.7 0.8 copy-done.9
  91.5 1.7 %convolution_convert_fusion.2 = bf16[256,1024]{1,0:T(8,128)(2,1)} fusion(bf16[256,1152]{1,0:T(8,128)(2,1)S(1)} %copy-done.9, bf16[1152,1024]{1,0:T(8,128)(2,1)S(1)} %bitcast.14), kind=kOutput, calls=%fused_computation.3 | convolution fusion | flops 604241920 | bytes 3473408 | tf_op jit(solution)/shard_map/dot_general | solution.py:82
  93.2 4.5 %collective-permute-start.4 = (bf16[256,1024]{1,0:T(8,128)(2,1)}, bf16[256,1024]{1,0:T(8,128)(2,1)S(1)}, u32[]{:S(2)}, u32[]{:S(2)}) collective-permute-start(bf16[256,1024]{1,0:T(8,128)(2,1)} %convolution_convert_fusion.2), channel_id=1, source_target_pairs={{0,8},{4,12},{8,0},{12,4},{1,9},{5,13},{9,1},{13,5},{2,10},{6,14},... | collective-permute-start | bytes 1572872 | tf_op jit(solution)/shard_map/ppermute | solution.py:45
  97.7 1.6 %convolution_convert_fusion.1 = bf16[256,1024]{1,0:T(8,128)(2,1)} fusion(bf16[256,1152]{1,0:T(8,128)(2,1)S(1)} %copy-done.7, bf16[1152,1024]{1,0:T(8,128)(2,1)S(1)} %bitcast.15), kind=kOutput, calls=%fused_computation.2 | convolution fusion | flops 604241920 | bytes 3473408 | tf_op jit(solution)/shard_map/dot_general | solution.py:82
  99.3 3.2 %collective-permute-start.5 = (bf16[256,1024]{1,0:T(8,128)(2,1)}, bf16[256,1024]{1,0:T(8,128)(2,1)S(1)}, u32[]{:S(2)}, u32[]{:S(2)}) collective-permute-start(bf16[256,1024]{1,0:T(8,128)(2,1)} %convolution_convert_fusion.1), channel_id=1, source_target_pairs={{0,12},{4,0},{8,4},{12,8},{1,13},{5,1},{9,5},{13,9},{2,14},{6,2},{... | collective-permute-start | bytes 1572872 | tf_op jit(solution)/shard_map/ppermute | solution.py:45
  102.5 1.6 %convolution_convert_fusion = bf16[256,1024]{1,0:T(8,128)(2,1)} fusion(bf16[256,1152]{1,0:T(8,128)(2,1)S(1)} %copy-done.5, bf16[1152,1024]{1,0:T(8,128)(2,1)S(1)} %bitcast.16), kind=kOutput, calls=%fused_computation.1 | convolution fusion | flops 604241920 | bytes 3473408 | tf_op jit(solution)/shard_map/dot_general | solution.py:82
  104.1 2.2 %collective-permute-start.6 = (bf16[256,1024]{1,0:T(8,128)(2,1)}, bf16[256,1024]{1,0:T(8,128)(2,1)}, u32[]{:S(2)}, u32[]{:S(2)}) collective-permute-start(bf16[256,1024]{1,0:T(8,128)(2,1)} %convolution_convert_fusion), channel_id=1, source_target_pairs={{0,4},{4,8},{8,12},{12,0},{1,5},{5,9},{9,13},{13,1},{2,6},{6,10},{... | collective-permute-start | bytes 1572872 | tf_op jit(solution)/shard_map/ppermute | solution.py:45
  106.4 0.6 reshape.33
  107.0 0.6 reshape.34
  107.7 1.9 %fusion = f32[256,1024]{1,0:T(8,128)S(1)} fusion(bf16[1152,1024]{1,0:T(8,128)(2,1)S(1)} %bitcast.17, bf16[256,4608]{1,0:T(8,128)(2,1)} %param.4, s32[]{:T(128)S(6)} %select_n.24), kind=kOutput, calls=%fused_computation.7 | convolution fusion | flops 603979776 | bytes 3997700 | tf_op jit(solution)/shard_map/dot_general | solution.py:80
  109.6 0.4 collective-permute-done.4
  110.0 11.7 %collective-permute-done.5 = bf16[256,1024]{1,0:T(8,128)(2,1)S(1)} collective-permute-done((bf16[256,1024]{1,0:T(8,128)(2,1)}, bf16[256,1024]{1,0:T(8,128)(2,1)S(1)}, u32[]{:S(2)}, u32[]{:S(2)}) %collective-permute-start.5) | collective-permute-done | bytes 524320 | tf_op jit(solution)/shard_map/ppermute | solution.py:45
  121.7 2.2 %multiply_convert_fusion = bf16[256,1024]{1,0:T(8,128)(2,1)} fusion(bf16[256,1024]{1,0:T(8,128)(2,1)} %collective-permute-done.6, bf16[256,1024]{1,0:T(8,128)(2,1)S(1)} %collective-permute-done.5, f32[256,1024]{1,0:T(8,128)S(1)} %fusion, bf16[256,1024]{1,0:T(8,128)(2,1)S(1)} %collective-permute-done.4), kind=kLoop, calls=%fused_computation.6 | loop fusion | flops 2097152 | bytes 3145728 | tf_op jit(solution)/shard_map/convert_element_type | solution.py:84
  (22 shorter events, 0.4 us)
Async XLA Ops:
  0.6 16.6 %copy-start.1 = (bf16[256,4608]{1,0:T(8,128)(2,1)S(1)}, bf16[256,4608]{1,0:T(8,128)(2,1)}, u32[]{:S(2)}) copy-start(bf16[256,4608]{1,0:T(8,128)(2,1)} %param.4) | copy-start | bytes 7077892
  2.9 34.3 %all-to-all-start = ((bf16[32,72,128]{2,1,0:T(8,128)(2,1)}), bf16[32,72,128]{2,1,0:T(8,128)(2,1)S(1)}, u32[]{:S(2)}, u32[]{:S(2)}) async-start(bf16[32,72,128]{2,1,0:T(8,128)(2,1)} %reshape.28), calls=%async_computation | async-start | bytes 1179648 | tf_op jit(solution)/shard_map/all_to_all | solution.py:56
  18.4 17.2 %collective-permute-start = (bf16[256,1152]{1,0:T(8,128)(2,1)}, bf16[256,1152]{1,0:T(8,128)(2,1)S(1)}, u32[]{:S(2)}, u32[]{:S(2)}) collective-permute-start(bf16[256,1152]{1,0:T(8,128)(2,1)} %get-tuple-element.22), channel_id=1, source_target_pairs={{0,4},{4,8},{8,12},{12,0},{1,5},{5,9},{9,13},{13,1},{2,6},{6,10},{... | collective-permute-start | bytes 1769480 | tf_op jit(solution)/shard_map/ppermute | solution.py:45
  21.5 15.7 %collective-permute-start.1 = (bf16[256,1152]{1,0:T(8,128)(2,1)}, bf16[256,1152]{1,0:T(8,128)(2,1)S(1)}, u32[]{:S(2)}, u32[]{:S(2)}) collective-permute-start(bf16[256,1152]{1,0:T(8,128)(2,1)} %get-tuple-element.23), channel_id=1, source_target_pairs={{0,12},{4,0},{8,4},{12,8},{1,13},{5,1},{9,5},{13,9},{2,14},{6,2},{... | collective-permute-start | bytes 1769480 | tf_op jit(solution)/shard_map/ppermute | solution.py:45
  35.6 6.6 %copy-start.6 = (bf16[256,1152]{1,0:T(8,128)(2,1)}, bf16[256,1152]{1,0:T(8,128)(2,1)S(1)}, u32[]{:S(2)}) copy-start(bf16[256,1152]{1,0:T(8,128)(2,1)S(1)} %collective-permute-done) | copy-start | bytes 1769476
  37.2 30.4 %copy-start.4 = (bf16[256,1152]{1,0:T(8,128)(2,1)}, bf16[256,1152]{1,0:T(8,128)(2,1)S(1)}, u32[]{:S(2)}) copy-start(bf16[256,1152]{1,0:T(8,128)(2,1)S(1)} %collective-permute-done.1) | copy-start | bytes 1769476
  37.2 0.9 copy-start
  42.2 38.5 %all-to-all-start.1 = ((bf16[64,72,128]{2,1,0:T(8,128)(2,1)}), bf16[64,72,128]{2,1,0:T(8,128)(2,1)S(1)}, u32[]{:S(2)}, u32[]{:S(2)}) async-start(bf16[64,72,128]{2,1,0:T(8,128)(2,1)} %broadcast_in_dim.2), calls=%async_computation.1 | async-start | bytes 2359296 | tf_op jit(solution)/shard_map/all_to_all | solution.py:70
  52.1 15.5 %collective-permute-start.2 = (bf16[256,1152]{1,0:T(8,128)(2,1)S(1)}, bf16[256,1152]{1,0:T(8,128)(2,1)S(1)}, u32[]{:S(2)}, u32[]{:S(2)}) collective-permute-start(bf16[256,1152]{1,0:T(8,128)(2,1)S(1)} %get-tuple-element.21), channel_id=1, source_target_pairs={{0,8},{4,12},{8,0},{12,4},{1,9},{5,13},{9,1},{13,5},{2,10},{6,14},... | collective-permute-start | bytes 1769480 | tf_op jit(solution)/shard_map/ppermute | solution.py:45
  67.6 22.8 %copy-start.8 = (bf16[256,1152]{1,0:T(8,128)(2,1)}, bf16[256,1152]{1,0:T(8,128)(2,1)S(1)}, u32[]{:S(2)}) copy-start(bf16[256,1152]{1,0:T(8,128)(2,1)S(1)} %collective-permute-done.2) | copy-start | bytes 1769476
  81.2 9.0 %collective-permute-start.3 = (bf16[2,288,1024]{2,1,0:T(8,128)(2,1)S(1)}, bf16[2,288,1024]{2,1,0:T(8,128)(2,1)S(1)}, u32[]{:S(2)}, u32[]{:S(2)}) collective-permute-start(bf16[2,288,1024]{2,1,0:T(8,128)(2,1)S(1)} %reshape.31), channel_id=1, source_target_pairs={{0,1},{1,0},{2,3},{3,2},{4,5},{5,4},{6,7},{7,6},{8,9},{9,8},{10,11... | collective-permute-start | bytes 3538952 | tf_op jit(solution)/shard_map/ppermute | solution.py:45
  90.4 1.1 copy-start.9
  90.6 7.0 %copy-start.7 = (bf16[256,1152]{1,0:T(8,128)(2,1)S(1)}, bf16[256,1152]{1,0:T(8,128)(2,1)}, u32[]{:S(2)}) copy-start(bf16[256,1152]{1,0:T(8,128)(2,1)} %copy-done.6) | copy-start | bytes 1769476
  93.2 9.3 %copy-start.5 = (bf16[256,1152]{1,0:T(8,128)(2,1)S(1)}, bf16[256,1152]{1,0:T(8,128)(2,1)}, u32[]{:S(2)}) copy-start(bf16[256,1152]{1,0:T(8,128)(2,1)} %copy-done.4) | copy-start | bytes 1769476
  93.2 16.9 %collective-permute-start.4 = (bf16[256,1024]{1,0:T(8,128)(2,1)}, bf16[256,1024]{1,0:T(8,128)(2,1)S(1)}, u32[]{:S(2)}, u32[]{:S(2)}) collective-permute-start(bf16[256,1024]{1,0:T(8,128)(2,1)} %convolution_convert_fusion.2), channel_id=1, source_target_pairs={{0,8},{4,12},{8,0},{12,4},{1,9},{5,13},{9,1},{13,5},{2,10},{6,14},... | collective-permute-start | bytes 1572872 | tf_op jit(solution)/shard_map/ppermute | solution.py:45
  99.3 7.1 %copy-start.3 = (f32[72,128]{1,0:T(8,128)S(1)}, f32[72,128]{1,0:T(8,128)}, u32[]{:S(2)}) copy-start(f32[72,128]{1,0:T(8,128)} %get-tuple-element.17) | copy-start | bytes 110596
  99.3 7.7 %copy-start.2 = (f32[72,128]{1,0:T(8,128)S(1)}, f32[72,128]{1,0:T(8,128)}, u32[]{:S(2)}) copy-start(f32[72,128]{1,0:T(8,128)} %get-tuple-element.18) | copy-start | bytes 110596
  99.3 22.4 %collective-permute-start.5 = (bf16[256,1024]{1,0:T(8,128)(2,1)}, bf16[256,1024]{1,0:T(8,128)(2,1)S(1)}, u32[]{:S(2)}, u32[]{:S(2)}) collective-permute-start(bf16[256,1024]{1,0:T(8,128)(2,1)} %convolution_convert_fusion.1), channel_id=1, source_target_pairs={{0,12},{4,0},{8,4},{12,8},{1,13},{5,1},{9,5},{13,9},{2,14},{6,2},{... | collective-permute-start | bytes 1572872 | tf_op jit(solution)/shard_map/ppermute | solution.py:45
  104.1 17.6 %collective-permute-start.6 = (bf16[256,1024]{1,0:T(8,128)(2,1)}, bf16[256,1024]{1,0:T(8,128)(2,1)}, u32[]{:S(2)}, u32[]{:S(2)}) collective-permute-start(bf16[256,1024]{1,0:T(8,128)(2,1)} %convolution_convert_fusion), channel_id=1, source_target_pairs={{0,4},{4,8},{8,12},{12,0},{1,5},{5,9},{9,13},{13,1},{2,6},{6,10},{... | collective-permute-start | bytes 1572872 | tf_op jit(solution)/shard_map/ppermute | solution.py:45

commit v2 on v1

--- a/solution.py
+++ b/solution.py
@@ -10,6 +10,7 @@
 AXES = ("yl", "z", "x", "yh", "c")
 SIZES = (4, 8, 4, 2, 2)
 REPLICAS = 32
+CHIPS = 64
 ROWS = ("yh", "yl", "z")
 
 
@@ -27,7 +28,9 @@
     base_out = base - 0.7 * (outer_grad + 0.9 * momentum_out)
     mom_out_ref[...] = momentum_out
     base_out_ref[...] = base_out
-    frag_ref[...] = base_out.astype(jnp.bfloat16)
+    frag = base_out.astype(jnp.bfloat16)
+    for i in range(CHIPS):
+        frag_ref[i] = frag
 
 
 def outer_step(got, base, mom):
@@ -35,7 +38,7 @@
     f32 = jax.ShapeDtypeStruct((n, BLK), jnp.float32)
     return pl.pallas_call(
         outer_kernel,
-        out_shape=(f32, f32, jax.ShapeDtypeStruct((n, BLK), jnp.bfloat16)),
+        out_shape=(f32, f32, jax.ShapeDtypeStruct((CHIPS, n, BLK), jnp.bfloat16)),
         name="outer_step",
     )(got, base, mom)
 
@@ -61,15 +64,12 @@
         return lax.dynamic_slice_in_dim(activations, lax.rem(x + (by + nx), nx) * depth, depth, axis=1)
 
     acts = {by: shift(columns(by), "x", by) for by in (2, 1, -1)}
-    got, acts[1], acts[-1] = lax.optimization_barrier((got, acts[1], acts[-1]))
 
-    base_flat, mom_flat, frag = outer_step(
+    base_flat, mom_flat, copies = outer_step(
         got, base_master.reshape(flat, BLK), momentum.reshape(flat, BLK)
     )
-    pieces = 64
-    mine = lax.all_to_all(
-        jnp.broadcast_to(frag[None], (pieces, flat, BLK)), ROWS, split_axis=0, concat_axis=0, tiled=True
-    )
+    copies, acts[1], acts[-1] = lax.optimization_barrier((copies, acts[1], acts[-1]))
+    mine = lax.all_to_all(copies, ROWS, split_axis=0, concat_axis=0, tiled=True)
     mine, acts[2] = lax.optimization_barrier((mine, acts[2]))
     mine = mine.reshape(2, REPLICAS * owned, width)
     other = shift(mine, "c", 1)

time: 125 us -> 120 us (0.960)
  waiting for transfers between devices: 48.1 us -> 44.7 us
  local copies, waits for them, and re-layouts: 11.8 us -> 10.4 us
    ppermute x7, waiting for transfers between devices: 35.1 us -> 26 us  [shift(): return lax.ppermute(v, axis, [(i, (i + by) % n) for i in range(n)])]
    all_to_all x1, waiting for transfers between devices: 0.01 us -> 5.59 us  [body(): lax.all_to_all(inner_weights.reshape(REPLICAS, flat, BLK), ('yl', 'z'), s...]
    broadcast_in_dim x1 -> x0, local copies, waits for them, and re-layouts: 1.9 us -> none  [body(): jnp.broadcast_to(frag[None], (pieces, flat, BLK))]
  transfers between devices with their start and end apart: 9 -> 9, of which waited for: 7 -> 7; matrix products, arithmetic and copies ran while one was open for 9% -> 9% of each run, Pallas kernels for 0% -> 2%
where the time goes in v2:
time: 120 us; the launch traced here: 119 us
  starting transfers between devices  51 us (42%)
  waiting for transfers between devices  44.7 us (37%)
  local copies, waits for them, and re-layouts  10.4 us (9%)
  matrix products  6.86 us (6%)
  Pallas kernels  2.65 us (2%)
  other arithmetic  2.57 us (2%)
    ppermute x7, starting transfers between devices, shift(): return lax.ppermute(v, axis, [(i, (i + by) % n) for i in range(n)])  27.3 us
    ppermute x7, waiting for transfers between devices, shift(): return lax.ppermute(v, axis, [(i, (i + by) % n) for i in range(n)])  26 us
    all_to_all x1, starting transfers between devices, body(): lax.all_to_all(inner_weights.reshape(REPLICAS, flat, BLK), ('yl', 'z'), s...  14.3 us
    all_to_all x1, waiting for transfers between devices, body(): mine = lax.all_to_all(copies, ROWS, split_axis=0, concat_axis=0, tiled=True)  13.1 us
    all_to_all x1, starting transfers between devices, body(): mine = lax.all_to_all(copies, ROWS, split_axis=0, concat_axis=0, tiled=True)  9.39 us
    all_to_all x1, waiting for transfers between devices, body(): lax.all_to_all(inner_weights.reshape(REPLICAS, flat, BLK), ('yl', 'z'), s...  5.59 us
    dot_general x3, matrix products, body(): jnp.dot(acts[by], rows, preferred_element_type=jnp.float32)  4.96 us
    pallas_call x1, Pallas kernels, outer_step(): pl.pallas_call(outer_kernel, out_shape=(f32, f32, jax.ShapeDtypeStruct((C...  2.65 us
  transfers between devices with their start and end apart: 9, of which 7 were waited for; matrix products, arithmetic and copies ran while one was open for 9% of the time, Pallas kernels for 2%

profile of v2, /device:TPU:1, one launch (start us, length us, event | category | flops | bytes accessed | tf_op | source)
XLA Modules:
  0.0 118.9 jit_solution(7816895715132768153)
XLA Ops:
  0.6 2.3 %reshape.27 = bf16[32,72,128]{2,1,0:T(8,128)(2,1)} reshape(bf16[1,288,1024]{2,1,0:T(8,128)(2,1)} %param.7) | data formatting | bytes 1179648 | tf_op jit(solution)/shard_map/reshape | solution.py:60
  2.9 14.3 %all-to-all-start = ((bf16[32,72,128]{2,1,0:T(8,128)(2,1)}), bf16[32,72,128]{2,1,0:T(8,128)(2,1)S(1)}, u32[]{:S(2)}, u32[]{:S(2)}) async-start(bf16[32,72,128]{2,1,0:T(8,128)(2,1)} %reshape.27), calls=%async_computation | async-start | bytes 1179648 | tf_op jit(solution)/shard_map/all_to_all | solution.py:59
  17.2 1.2 constant_dynamic-slice_fusion
  18.4 3.1 %collective-permute-start = (bf16[256,1152]{1,0:T(8,128)(2,1)}, bf16[256,1152]{1,0:T(8,128)(2,1)S(1)}, u32[]{:S(2)}, u32[]{:S(2)}) collective-permute-start(bf16[256,1152]{1,0:T(8,128)(2,1)} %get-tuple-element.22), channel_id=1, source_target_pairs={{0,4},{4,8},{8,12},{12,0},{1,5},{5,9},{9,13},{13,1},{2,6},{6,10},{... | collective-permute-start | bytes 1769480 | tf_op jit(solution)/shard_map/ppermute | solution.py:48
  21.5 3.4 %collective-permute-start.1 = (bf16[256,1152]{1,0:T(8,128)(2,1)}, bf16[256,1152]{1,0:T(8,128)(2,1)S(1)}, u32[]{:S(2)}, u32[]{:S(2)}) collective-permute-start(bf16[256,1152]{1,0:T(8,128)(2,1)} %get-tuple-element.23), channel_id=1, source_target_pairs={{0,12},{4,0},{8,4},{12,8},{1,13},{5,1},{9,5},{13,9},{2,14},{6,2},{... | collective-permute-start | bytes 1769480 | tf_op jit(solution)/shard_map/ppermute | solution.py:48
  24.9 1.5 %reshape.28.base_ref = f32[72,128]{1,0:T(8,128)} reshape(f32[9,1024]{1,0:T(8,128)} %param.5) | data formatting | bytes 73728 | tf_op jit(solution)/shard_map/reshape | solution.py:69
  26.4 1.5 %reshape.29.mom_ref = f32[72,128]{1,0:T(8,128)} reshape(f32[9,1024]{1,0:T(8,128)} %param.6) | data formatting | bytes 73728 | tf_op jit(solution)/shard_map/reshape | solution.py:69
  27.8 5.6 %all-to-all-done.inner_ref = bf16[32,72,128]{2,1,0:T(8,128)(2,1)S(1)} async-done(((bf16[32,72,128]{2,1,0:T(8,128)(2,1)}), bf16[32,72,128]{2,1,0:T(8,128)(2,1)S(1)}, u32[]{:S(2)}, u32[]{:S(2)}) %all-to-all-start) | async-done | bytes 589856 | tf_op jit(solution)/shard_map/all_to_all | solution.py:59
  33.4 0.8 copy-done
  34.3 2.6 %outer_step.1 = (f32[72,128]{1,0:T(8,128)}, f32[72,128]{1,0:T(8,128)}, bf16[64,72,128]{2,1,0:T(8,128)(2,1)}) custom-call(bf16[32,72,128]{2,1,0:T(8,128)(2,1)} %copy-done, f32[72,128]{1,0:T(8,128)} %reshape.28.base_ref, f32[72,128]{1,0:T(8,128)} %reshape.29.mom_ref), custom_call_target="tpu_custom_call" | custom-call | tf_op jit(solution)/shard_map/outer_step/pallas_call | solution.py:39
  36.9 0.3 collective-permute-done.1
  37.2 0.5 copy-done.6
  37.7 9.4 %all-to-all-start.1 = ((bf16[64,72,128]{2,1,0:T(8,128)(2,1)}), bf16[64,72,128]{2,1,0:T(8,128)(2,1)S(1)}, u32[]{:S(2)}, u32[]{:S(2)}) async-start(bf16[64,72,128]{2,1,0:T(8,128)(2,1)} %get-tuple-element.12), calls=%async_computation.1 | async-start | bytes 2359296 | tf_op jit(solution)/shard_map/all_to_all | solution.py:72
  47.1 4.4 %collective-permute-start.2 = (bf16[256,1152]{1,0:T(8,128)(2,1)S(1)}, bf16[256,1152]{1,0:T(8,128)(2,1)S(1)}, u32[]{:S(2)}, u32[]{:S(2)}) collective-permute-start(bf16[256,1152]{1,0:T(8,128)(2,1)S(1)} %get-tuple-element.21), channel_id=1, source_target_pairs={{0,8},{4,12},{8,0},{12,4},{1,9},{5,13},{9,1},{13,5},{2,10},{6,14},... | collective-permute-start | bytes 1769480 | tf_op jit(solution)/shard_map/ppermute | solution.py:48
  51.5 11.1 %collective-permute-done.2 = bf16[256,1152]{1,0:T(8,128)(2,1)S(1)} collective-permute-done((bf16[256,1152]{1,0:T(8,128)(2,1)S(1)}, bf16[256,1152]{1,0:T(8,128)(2,1)S(1)}, u32[]{:S(2)}, u32[]{:S(2)}) %collective-permute-start.2) | collective-permute-done | bytes 589856 | tf_op jit(solution)/shard_map/ppermute | solution.py:48
  62.6 13.1 %all-to-all-done.1 = bf16[64,72,128]{2,1,0:T(8,128)(2,1)S(1)} async-done(((bf16[64,72,128]{2,1,0:T(8,128)(2,1)}), bf16[64,72,128]{2,1,0:T(8,128)(2,1)S(1)}, u32[]{:S(2)}, u32[]{:S(2)}) %all-to-all-start.1) | async-done | bytes 1179680 | tf_op jit(solution)/shard_map/all_to_all | solution.py:72
  75.7 0.5 reshape.30
  76.2 6.6 %collective-permute-start.3 = (bf16[2,288,1024]{2,1,0:T(8,128)(2,1)S(1)}, bf16[2,288,1024]{2,1,0:T(8,128)(2,1)S(1)}, u32[]{:S(2)}, u32[]{:S(2)}) collective-permute-start(bf16[2,288,1024]{2,1,0:T(8,128)(2,1)S(1)} %reshape.30), channel_id=1, source_target_pairs={{0,1},{1,0},{2,3},{3,2},{4,5},{5,4},{6,7},{7,6},{8,9},{9,8},{10,11... | collective-permute-start | bytes 3538952 | tf_op jit(solution)/shard_map/ppermute | solution.py:48
  82.8 2.4 %collective-permute-done.3 = bf16[2,288,1024]{2,1,0:T(8,128)(2,1)S(1)} collective-permute-done((bf16[2,288,1024]{2,1,0:T(8,128)(2,1)S(1)}, bf16[2,288,1024]{2,1,0:T(8,128)(2,1)S(1)}, u32[]{:S(2)}, u32[]{:S(2)}) %collective-permute-start.3) | collective-permute-done | bytes 1179680 | tf_op jit(solution)/shard_map/ppermute | solution.py:48
  85.7 0.8 copy-done.9
  86.5 1.7 %convolution_convert_fusion.2 = bf16[256,1024]{1,0:T(8,128)(2,1)} fusion(bf16[256,1152]{1,0:T(8,128)(2,1)S(1)} %copy-done.9, bf16[1152,1024]{1,0:T(8,128)(2,1)S(1)} %bitcast.14), kind=kOutput, calls=%fused_computation.3 | convolution fusion | flops 604241920 | bytes 3473408 | tf_op jit(solution)/shard_map/dot_general | solution.py:82
  88.2 4.5 %collective-permute-start.4 = (bf16[256,1024]{1,0:T(8,128)(2,1)}, bf16[256,1024]{1,0:T(8,128)(2,1)S(1)}, u32[]{:S(2)}, u32[]{:S(2)}) collective-permute-start(bf16[256,1024]{1,0:T(8,128)(2,1)} %convolution_convert_fusion.2), channel_id=1, source_target_pairs={{0,8},{4,12},{8,0},{12,4},{1,9},{5,13},{9,1},{13,5},{2,10},{6,14},... | collective-permute-start | bytes 1572872 | tf_op jit(solution)/shard_map/ppermute | solution.py:48
  92.7 1.6 %convolution_convert_fusion.1 = bf16[256,1024]{1,0:T(8,128)(2,1)} fusion(bf16[256,1152]{1,0:T(8,128)(2,1)S(1)} %copy-done.7, bf16[1152,1024]{1,0:T(8,128)(2,1)S(1)} %bitcast.15), kind=kOutput, calls=%fused_computation.2 | convolution fusion | flops 604241920 | bytes 3473408 | tf_op jit(solution)/shard_map/dot_general | solution.py:82
  94.3 3.2 %collective-permute-start.5 = (bf16[256,1024]{1,0:T(8,128)(2,1)}, bf16[256,1024]{1,0:T(8,128)(2,1)S(1)}, u32[]{:S(2)}, u32[]{:S(2)}) collective-permute-start(bf16[256,1024]{1,0:T(8,128)(2,1)} %convolution_convert_fusion.1), channel_id=1, source_target_pairs={{0,12},{4,0},{8,4},{12,8},{1,13},{5,1},{9,5},{13,9},{2,14},{6,2},{... | collective-permute-start | bytes 1572872 | tf_op jit(solution)/shard_map/ppermute | solution.py:48
  97.5 1.6 %convolution_convert_fusion = bf16[256,1024]{1,0:T(8,128)(2,1)} fusion(bf16[256,1152]{1,0:T(8,128)(2,1)S(1)} %copy-done.5, bf16[1152,1024]{1,0:T(8,128)(2,1)S(1)} %bitcast.16), kind=kOutput, calls=%fused_computation.1 | convolution fusion | flops 604241920 | bytes 3473408 | tf_op jit(solution)/shard_map/dot_general | solution.py:82
  99.2 2.2 %collective-permute-start.6 = (bf16[256,1024]{1,0:T(8,128)(2,1)}, bf16[256,1024]{1,0:T(8,128)(2,1)}, u32[]{:S(2)}, u32[]{:S(2)}) collective-permute-start(bf16[256,1024]{1,0:T(8,128)(2,1)} %convolution_convert_fusion), channel_id=1, source_target_pairs={{0,4},{4,8},{8,12},{12,0},{1,5},{5,9},{9,13},{13,1},{2,6},{6,10},{... | collective-permute-start | bytes 1572872 | tf_op jit(solution)/shard_map/ppermute | solution.py:48
  101.4 0.6 reshape.32
  102.1 0.6 reshape.33
  102.7 1.9 %fusion = f32[256,1024]{1,0:T(8,128)S(1)} fusion(bf16[1152,1024]{1,0:T(8,128)(2,1)S(1)} %bitcast.17, bf16[256,4608]{1,0:T(8,128)(2,1)} %param.4, s32[]{:T(128)S(6)} %select_n.24), kind=kOutput, calls=%fused_computation.7 | convolution fusion | flops 603979776 | bytes 3997700 | tf_op jit(solution)/shard_map/dot_general | solution.py:80
  104.6 0.4 collective-permute-done.4
  105.0 11.7 %collective-permute-done.5 = bf16[256,1024]{1,0:T(8,128)(2,1)S(1)} collective-permute-done((bf16[256,1024]{1,0:T(8,128)(2,1)}, bf16[256,1024]{1,0:T(8,128)(2,1)S(1)}, u32[]{:S(2)}, u32[]{:S(2)}) %collective-permute-start.5) | collective-permute-done | bytes 524320 | tf_op jit(solution)/shard_map/ppermute | solution.py:48
  116.7 2.2 %multiply_convert_fusion = bf16[256,1024]{1,0:T(8,128)(2,1)} fusion(bf16[256,1024]{1,0:T(8,128)(2,1)} %collective-permute-done.6, bf16[256,1024]{1,0:T(8,128)(2,1)S(1)} %collective-permute-done.5, f32[256,1024]{1,0:T(8,128)S(1)} %fusion, bf16[256,1024]{1,0:T(8,128)(2,1)S(1)} %collective-permute-done.4), kind=kLoop, calls=%fused_computation.6 | loop fusion | flops 2097152 | bytes 3145728 | tf_op jit(solution)/shard_map/convert_element_type | solution.py:84
  (21 shorter events, 0.4 us)
Async XLA Ops:
  0.6 16.6 %copy-start.1 = (bf16[256,4608]{1,0:T(8,128)(2,1)S(1)}, bf16[256,4608]{1,0:T(8,128)(2,1)}, u32[]{:S(2)}) copy-start(bf16[256,4608]{1,0:T(8,128)(2,1)} %param.4) | copy-start | bytes 7077892
  2.9 30.5 %all-to-all-start = ((bf16[32,72,128]{2,1,0:T(8,128)(2,1)}), bf16[32,72,128]{2,1,0:T(8,128)(2,1)S(1)}, u32[]{:S(2)}, u32[]{:S(2)}) async-start(bf16[32,72,128]{2,1,0:T(8,128)(2,1)} %reshape.27), calls=%async_computation | async-start | bytes 1179648 | tf_op jit(solution)/shard_map/all_to_all | solution.py:59
  18.4 18.5 %collective-permute-start = (bf16[256,1152]{1,0:T(8,128)(2,1)}, bf16[256,1152]{1,0:T(8,128)(2,1)S(1)}, u32[]{:S(2)}, u32[]{:S(2)}) collective-permute-start(bf16[256,1152]{1,0:T(8,128)(2,1)} %get-tuple-element.22), channel_id=1, source_target_pairs={{0,4},{4,8},{8,12},{12,0},{1,5},{5,9},{9,13},{13,1},{2,6},{6,10},{... | collective-permute-start | bytes 1769480 | tf_op jit(solution)/shard_map/ppermute | solution.py:48
  21.5 15.7 %collective-permute-start.1 = (bf16[256,1152]{1,0:T(8,128)(2,1)}, bf16[256,1152]{1,0:T(8,128)(2,1)S(1)}, u32[]{:S(2)}, u32[]{:S(2)}) collective-permute-start(bf16[256,1152]{1,0:T(8,128)(2,1)} %get-tuple-element.23), channel_id=1, source_target_pairs={{0,12},{4,0},{8,4},{12,8},{1,13},{5,1},{9,5},{13,9},{2,14},{6,2},{... | collective-permute-start | bytes 1769480 | tf_op jit(solution)/shard_map/ppermute | solution.py:48
  33.4 0.8 copy-start
  36.9 0.8 copy-start.6
  37.2 25.4 %copy-start.4 = (bf16[256,1152]{1,0:T(8,128)(2,1)}, bf16[256,1152]{1,0:T(8,128)(2,1)S(1)}, u32[]{:S(2)}) copy-start(bf16[256,1152]{1,0:T(8,128)(2,1)S(1)} %collective-permute-done.1) | copy-start | bytes 1769476
  37.7 38.0 %all-to-all-start.1 = ((bf16[64,72,128]{2,1,0:T(8,128)(2,1)}), bf16[64,72,128]{2,1,0:T(8,128)(2,1)S(1)}, u32[]{:S(2)}, u32[]{:S(2)}) async-start(bf16[64,72,128]{2,1,0:T(8,128)(2,1)} %get-tuple-element.12), calls=%async_computation.1 | async-start | bytes 2359296 | tf_op jit(solution)/shard_map/all_to_all | solution.py:72
  47.1 15.5 %collective-permute-start.2 = (bf16[256,1152]{1,0:T(8,128)(2,1)S(1)}, bf16[256,1152]{1,0:T(8,128)(2,1)S(1)}, u32[]{:S(2)}, u32[]{:S(2)}) collective-permute-start(bf16[256,1152]{1,0:T(8,128)(2,1)S(1)} %get-tuple-element.21), channel_id=1, source_target_pairs={{0,8},{4,12},{8,0},{12,4},{1,9},{5,13},{9,1},{13,5},{2,10},{6,14},... | collective-permute-start | bytes 1769480 | tf_op jit(solution)/shard_map/ppermute | solution.py:48
  62.6 22.8 %copy-start.8 = (bf16[256,1152]{1,0:T(8,128)(2,1)}, bf16[256,1152]{1,0:T(8,128)(2,1)S(1)}, u32[]{:S(2)}) copy-start(bf16[256,1152]{1,0:T(8,128)(2,1)S(1)} %collective-permute-done.2) | copy-start | bytes 1769476
  76.2 9.0 %collective-permute-start.3 = (bf16[2,288,1024]{2,1,0:T(8,128)(2,1)S(1)}, bf16[2,288,1024]{2,1,0:T(8,128)(2,1)S(1)}, u32[]{:S(2)}, u32[]{:S(2)}) collective-permute-start(bf16[2,288,1024]{2,1,0:T(8,128)(2,1)S(1)} %reshape.30), channel_id=1, source_target_pairs={{0,1},{1,0},{2,3},{3,2},{4,5},{5,4},{6,7},{7,6},{8,9},{9,8},{10,11... | collective-permute-start | bytes 3538952 | tf_op jit(solution)/shard_map/ppermute | solution.py:48
  85.4 1.1 copy-start.9
  85.7 7.0 %copy-start.7 = (bf16[256,1152]{1,0:T(8,128)(2,1)S(1)}, bf16[256,1152]{1,0:T(8,128)(2,1)}, u32[]{:S(2)}) copy-start(bf16[256,1152]{1,0:T(8,128)(2,1)} %copy-done.6) | copy-start | bytes 1769476
  88.2 9.3 %copy-start.5 = (bf16[256,1152]{1,0:T(8,128)(2,1)S(1)}, bf16[256,1152]{1,0:T(8,128)(2,1)}, u32[]{:S(2)}) copy-start(bf16[256,1152]{1,0:T(8,128)(2,1)} %copy-done.4) | copy-start | bytes 1769476
  88.2 16.9 %collective-permute-start.4 = (bf16[256,1024]{1,0:T(8,128)(2,1)}, bf16[256,1024]{1,0:T(8,128)(2,1)S(1)}, u32[]{:S(2)}, u32[]{:S(2)}) collective-permute-start(bf16[256,1024]{1,0:T(8,128)(2,1)} %convolution_convert_fusion.2), channel_id=1, source_target_pairs={{0,8},{4,12},{8,0},{12,4},{1,9},{5,13},{9,1},{13,5},{2,10},{6,14},... | collective-permute-start | bytes 1572872 | tf_op jit(solution)/shard_map/ppermute | solution.py:48
  94.3 7.1 %copy-start.3 = (f32[72,128]{1,0:T(8,128)S(1)}, f32[72,128]{1,0:T(8,128)}, u32[]{:S(2)}) copy-start(f32[72,128]{1,0:T(8,128)} %get-tuple-element.17) | copy-start | bytes 110596
  94.3 7.7 %copy-start.2 = (f32[72,128]{1,0:T(8,128)S(1)}, f32[72,128]{1,0:T(8,128)}, u32[]{:S(2)}) copy-start(f32[72,128]{1,0:T(8,128)} %get-tuple-element.18) | copy-start | bytes 110596
  94.3 22.4 %collective-permute-start.5 = (bf16[256,1024]{1,0:T(8,128)(2,1)}, bf16[256,1024]{1,0:T(8,128)(2,1)S(1)}, u32[]{:S(2)}, u32[]{:S(2)}) collective-permute-start(bf16[256,1024]{1,0:T(8,128)(2,1)} %convolution_convert_fusion.1), channel_id=1, source_target_pairs={{0,12},{4,0},{8,4},{12,8},{1,13},{5,1},{9,5},{13,9},{2,14},{6,2},{... | collective-permute-start | bytes 1572872 | tf_op jit(solution)/shard_map/ppermute | solution.py:48
  99.2 17.6 %collective-permute-start.6 = (bf16[256,1024]{1,0:T(8,128)(2,1)}, bf16[256,1024]{1,0:T(8,128)(2,1)}, u32[]{:S(2)}, u32[]{:S(2)}) collective-permute-start(bf16[256,1024]{1,0:T(8,128)(2,1)} %convolution_convert_fusion), channel_id=1, source_target_pairs={{0,4},{4,8},{8,12},{12,0},{1,5},{5,9},{9,13},{13,1},{2,6},{6,10},{... | collective-permute-start | bytes 1572872 | tf_op jit(solution)/shard_map/ppermute | solution.py:48

commit v3 on v2

--- a/solution.py
+++ b/solution.py
@@ -39,8 +39,26 @@
     return pl.pallas_call(
         outer_kernel,
         out_shape=(f32, f32, jax.ShapeDtypeStruct((CHIPS, n, BLK), jnp.bfloat16)),
+        compiler_params=pltpu.CompilerParams(vmem_limit_bytes=8 * 2**20),
         name="outer_step",
     )(got, base, mom)
+
+
+def sum_kernel(own_ref, *refs):
+    *part_refs, keys_ref = refs
+    total = own_ref[...]
+    for part_ref in part_refs:
+        total = total + part_ref[...].astype(jnp.float32)
+    keys_ref[...] = (total * D ** (-0.5)).astype(jnp.bfloat16)
+
+
+def sum_parts(own, parts):
+    return pl.pallas_call(
+        sum_kernel,
+        out_shape=jax.ShapeDtypeStruct(own.shape, jnp.bfloat16),
+        compiler_params=pltpu.CompilerParams(vmem_limit_bytes=8 * 2**20),
+        name="sum_parts",
+    )(own, *parts)
 
 
 def shift(v, axis, by):
@@ -68,20 +86,25 @@
     base_flat, mom_flat, copies = outer_step(
         got, base_master.reshape(flat, BLK), momentum.reshape(flat, BLK)
     )
-    copies, acts[1], acts[-1] = lax.optimization_barrier((copies, acts[1], acts[-1]))
+    copies, acts[1] = lax.optimization_barrier((copies, acts[1]))
     mine = lax.all_to_all(copies, ROWS, split_axis=0, concat_axis=0, tiled=True)
-    mine, acts[2] = lax.optimization_barrier((mine, acts[2]))
+    mine, acts[2], acts[-1] = lax.optimization_barrier((mine, acts[2], acts[-1]))
     mine = mine.reshape(2, REPLICAS * owned, width)
     other = shift(mine, "c", 1)
     first = jnp.where(c == 0, mine, other)
     second = jnp.where(c == 0, other, mine)
     rows = jnp.stack([first, second], axis=1).reshape(depth, width)
 
-    total = jnp.dot(columns(0), rows, preferred_element_type=jnp.float32)
-    for by in (2, 1, -1):
-        part = jnp.dot(acts[by], rows, preferred_element_type=jnp.float32).astype(jnp.bfloat16)
-        total = total + shift(part, "x", -by).astype(jnp.float32)
-    keys = (total * D ** (-0.5)).astype(jnp.bfloat16)
+    def product(a):
+        return jnp.dot(a, rows, preferred_element_type=jnp.float32)
+
+    far = product(acts[2]).astype(jnp.bfloat16)
+    far, acts[1], acts[-1] = lax.optimization_barrier((far, acts[1], acts[-1]))
+    own = product(columns(0))
+    near = [shift(product(acts[by]).astype(jnp.bfloat16), "x", -by) for by in (1, -1)]
+    own = own + shift(far, "x", -2).astype(jnp.float32)
+    own, *near = lax.optimization_barrier((own, *near))
+    keys = sum_parts(own, near)
     return keys, base_flat.reshape(owned, width), mom_flat.reshape(owned, width)
 
 

time: 120 us -> 118 us (0.983)
  waiting for transfers between devices: 44.7 us -> 47.3 us
  other arithmetic: 2.57 us -> 0.38 us
  starting transfers between devices: 51 us -> 49.7 us
    all_to_all x1, waiting for transfers between devices: 13.1 us -> 0.01 us  [body(): mine = lax.all_to_all(copies, ROWS, split_axis=0, concat_axis=0, tiled=True)]
    ppermute x7, waiting for transfers between devices: 26 us -> 37.2 us  [shift(): return lax.ppermute(v, axis, [(i, (i + by) % n) for i in range(n)])]
    all_to_all x1, waiting for transfers between devices: 5.59 us -> 10.1 us  [body(): lax.all_to_all(inner_weights.reshape(REPLICAS, flat, BLK), ('yl', 'z'), s...]
    convert_element_type x1 -> x0, other arithmetic: 2.19 us -> none  [body(): keys = (total * D ** (-0.5)).astype(jnp.bfloat16)]
    ppermute x7, starting transfers between devices: 27.3 us -> 25.5 us  [shift(): return lax.ppermute(v, axis, [(i, (i + by) % n) for i in range(n)])]
    unnamed x20 -> x12, local copies, waits for them, and re-layouts: 2.2 us -> 2.5 us
  transfers between devices with their start and end apart: 9 -> 9, of which waited for: 7 -> 7; matrix products, arithmetic and copies ran while one was open for 9% -> 8% of each run, Pallas kernels for 2% -> 1%
where the time goes in v3:
time: 118 us; the launch traced here: 117 us
  starting transfers between devices  49.7 us (42%)
  waiting for transfers between devices  47.3 us (40%)
  local copies, waits for them, and re-layouts  9.42 us (8%)
  matrix products  7.16 us (6%)
  Pallas kernels  2.57 us (2%)
    ppermute x7, waiting for transfers between devices, shift(): return lax.ppermute(v, axis, [(i, (i + by) % n) for i in range(n)])  37.2 us
    ppermute x7, starting transfers between devices, shift(): return lax.ppermute(v, axis, [(i, (i + by) % n) for i in range(n)])  25.5 us
    all_to_all x1, starting transfers between devices, body(): lax.all_to_all(inner_weights.reshape(REPLICAS, flat, BLK), ('yl', 'z'), s...  14.3 us
    all_to_all x1, waiting for transfers between devices, body(): lax.all_to_all(inner_weights.reshape(REPLICAS, flat, BLK), ('yl', 'z'), s...  10.1 us
    all_to_all x1, starting transfers between devices, body(): mine = lax.all_to_all(copies, ROWS, split_axis=0, concat_axis=0, tiled=True)  9.9 us
    dot_general x4, matrix products, product(): return jnp.dot(a, rows, preferred_element_type=jnp.float32)  7.16 us
    unnamed x12, local copies, waits for them, and re-layouts  2.5 us
  transfers between devices with their start and end apart: 9, of which 7 were waited for; matrix products, arithmetic and copies ran while one was open for 8% of the time, Pallas kernels for 1%

profile of v3, /device:TPU:1, one launch (start us, length us, event | category | flops | bytes accessed | tf_op | source)
XLA Modules:
  0.0 117.3 jit_solution(13331955324419344883)
XLA Ops:
  0.6 2.2 %reshape.27 = bf16[32,72,128]{2,1,0:T(8,128)(2,1)} reshape(bf16[1,288,1024]{2,1,0:T(8,128)(2,1)} %param.7) | data formatting | bytes 1179648 | tf_op jit(solution)/shard_map/reshape | solution.py:78
  2.9 14.3 %all-to-all-start = ((bf16[32,72,128]{2,1,0:T(8,128)(2,1)}), bf16[32,72,128]{2,1,0:T(8,128)(2,1)S(1)}, u32[]{:S(2)}, u32[]{:S(2)}) async-start(bf16[32,72,128]{2,1,0:T(8,128)(2,1)} %reshape.27), calls=%async_computation | async-start | bytes 1179648 | tf_op jit(solution)/shard_map/all_to_all | solution.py:77
  17.2 1.2 constant_dynamic-slice_fusion
  18.4 3.2 %collective-permute-start = (bf16[256,1152]{1,0:T(8,128)(2,1)}, bf16[256,1152]{1,0:T(8,128)(2,1)S(1)}, u32[]{:S(2)}, u32[]{:S(2)}) collective-permute-start(bf16[256,1152]{1,0:T(8,128)(2,1)} %get-tuple-element.34), channel_id=1, source_target_pairs={{0,4},{4,8},{8,12},{12,0},{1,5},{5,9},{9,13},{13,1},{2,6},{6,10},{... | collective-permute-start | bytes 1769480 | tf_op jit(solution)/shard_map/ppermute | solution.py:66
  21.6 0.9 reshape.28.base_ref
  22.5 0.9 reshape.29.mom_ref
  23.3 10.1 %all-to-all-done.inner_ref = bf16[32,72,128]{2,1,0:T(8,128)(2,1)S(1)} async-done(((bf16[32,72,128]{2,1,0:T(8,128)(2,1)}), bf16[32,72,128]{2,1,0:T(8,128)(2,1)S(1)}, u32[]{:S(2)}, u32[]{:S(2)}) %all-to-all-start) | async-done | bytes 589856 | tf_op jit(solution)/shard_map/all_to_all | solution.py:77
  33.4 1.6 %outer_step.1 = (f32[72,128]{1,0:T(8,128)S(1)}, f32[72,128]{1,0:T(8,128)S(1)}, bf16[64,72,128]{2,1,0:T(8,128)(2,1)}) custom-call(bf16[32,72,128]{2,1,0:T(8,128)(2,1)S(1)} %all-to-all-done.inner_ref, f32[72,128]{1,0:T(8,128)S(1)} %reshape.28.base_ref, f32[72,128]{1,0:T(8,128)S(1)} %reshape.29.mom_ref), custom_call_target="tpu_custom_call" | custom-call | tf_op jit(solution)/shard_map/outer_step/pallas_call | solution.py:39
  35.0 0.7 collective-permute-done
  35.7 0.8 copy-done.2
  36.5 9.9 %all-to-all-start.1 = ((bf16[64,72,128]{2,1,0:T(8,128)(2,1)}), bf16[64,72,128]{2,1,0:T(8,128)(2,1)S(1)}, u32[]{:S(2)}, u32[]{:S(2)}) async-start(bf16[64,72,128]{2,1,0:T(8,128)(2,1)} %get-tuple-element.18), calls=%async_computation.1 | async-start | bytes 2359296 | tf_op jit(solution)/shard_map/all_to_all | solution.py:90
  46.4 3.4 %collective-permute-start.1 = (bf16[256,1152]{1,0:T(8,128)(2,1)S(1)}, bf16[256,1152]{1,0:T(8,128)(2,1)S(1)}, u32[]{:S(2)}, u32[]{:S(2)}) collective-permute-start(bf16[256,1152]{1,0:T(8,128)(2,1)S(1)} %copy-done.1), channel_id=1, source_target_pairs={{0,8},{4,12},{8,0},{12,4},{1,9},{5,13},{9,1},{13,5},{2,10},{6,14},... | collective-permute-start | bytes 1769480 | tf_op jit(solution)/shard_map/ppermute | solution.py:66
  49.9 2.8 %collective-permute-start.2 = (bf16[256,1152]{1,0:T(8,128)(2,1)S(1)}, bf16[256,1152]{1,0:T(8,128)(2,1)S(1)}, u32[]{:S(2)}, u32[]{:S(2)}) collective-permute-start(bf16[256,1152]{1,0:T(8,128)(2,1)S(1)} %get-tuple-element.33), channel_id=1, source_target_pairs={{0,12},{4,0},{8,4},{12,8},{1,13},{5,1},{9,5},{13,9},{2,14},{6,2},{... | collective-permute-start | bytes 1769480 | tf_op jit(solution)/shard_map/ppermute | solution.py:66
  52.7 9.6 %collective-permute-done.1 = bf16[256,1152]{1,0:T(8,128)(2,1)S(1)} collective-permute-done((bf16[256,1152]{1,0:T(8,128)(2,1)S(1)}, bf16[256,1152]{1,0:T(8,128)(2,1)S(1)}, u32[]{:S(2)}, u32[]{:S(2)}) %collective-permute-start.1) | collective-permute-done | bytes 589856 | tf_op jit(solution)/shard_map/ppermute | solution.py:66
  62.2 0.8 copy-done.4
  63.0 12.5 %collective-permute-done.2 = bf16[256,1152]{1,0:T(8,128)(2,1)S(1)} collective-permute-done((bf16[256,1152]{1,0:T(8,128)(2,1)S(1)}, bf16[256,1152]{1,0:T(8,128)(2,1)S(1)}, u32[]{:S(2)}, u32[]{:S(2)}) %collective-permute-start.2) | collective-permute-done | bytes 589856 | tf_op jit(solution)/shard_map/ppermute | solution.py:66
  75.6 0.5 reshape.30
  76.1 6.0 %collective-permute-start.3 = (bf16[2,288,1024]{2,1,0:T(8,128)(2,1)S(1)}, bf16[2,288,1024]{2,1,0:T(8,128)(2,1)S(1)}, u32[]{:S(2)}, u32[]{:S(2)}) collective-permute-start(bf16[2,288,1024]{2,1,0:T(8,128)(2,1)S(1)} %reshape.30), channel_id=1, source_target_pairs={{0,1},{1,0},{2,3},{3,2},{4,5},{5,4},{6,7},{7,6},{8,9},{9,8},{10,11... | collective-permute-start | bytes 3538952 | tf_op jit(solution)/shard_map/ppermute | solution.py:66
  82.2 2.4 %collective-permute-done.3 = bf16[2,288,1024]{2,1,0:T(8,128)(2,1)S(1)} collective-permute-done((bf16[2,288,1024]{2,1,0:T(8,128)(2,1)S(1)}, bf16[2,288,1024]{2,1,0:T(8,128)(2,1)S(1)}, u32[]{:S(2)}, u32[]{:S(2)}) %collective-permute-start.3) | collective-permute-done | bytes 1179680 | tf_op jit(solution)/shard_map/ppermute | solution.py:66
  85.0 0.8 copy-done.5
  85.8 1.7 %convolution_convert_fusion.2 = bf16[256,1024]{1,0:T(8,128)(2,1)} fusion(bf16[256,1152]{1,0:T(8,128)(2,1)S(1)} %copy-done.5, bf16[1152,1024]{1,0:T(8,128)(2,1)S(1)} %bitcast.14), kind=kOutput, calls=%fused_computation.3 | convolution fusion | flops 604241920 | bytes 3473408 | tf_op jit(solution)/shard_map/dot_general | solution.py:99
  87.5 3.6 %collective-permute-start.4 = (bf16[256,1024]{1,0:T(8,128)(2,1)}, bf16[256,1024]{1,0:T(8,128)(2,1)}, u32[]{:S(2)}, u32[]{:S(2)}) collective-permute-start(bf16[256,1024]{1,0:T(8,128)(2,1)} %convolution_convert_fusion.2), channel_id=1, source_target_pairs={{0,8},{4,12},{8,0},{12,4},{1,9},{5,13},{9,1},{13,5},{2,10},{6,14},... | collective-permute-start | bytes 1572872 | tf_op jit(solution)/shard_map/ppermute | solution.py:66
  91.1 1.7 %convolution_convert_fusion = bf16[256,1024]{1,0:T(8,128)(2,1)} fusion(bf16[256,1152]{1,0:T(8,128)(2,1)S(1)} %collective-permute-done.2, bf16[1152,1024]{1,0:T(8,128)(2,1)S(1)} %bitcast.15), kind=kOutput, calls=%fused_computation.1 | convolution fusion | flops 604241920 | bytes 3473408 | tf_op jit(solution)/shard_map/dot_general | solution.py:99
  92.8 2.2 %collective-permute-start.6 = (bf16[256,1024]{1,0:T(8,128)(2,1)}, bf16[256,1024]{1,0:T(8,128)(2,1)S(1)}, u32[]{:S(2)}, u32[]{:S(2)}) collective-permute-start(bf16[256,1024]{1,0:T(8,128)(2,1)} %convolution_convert_fusion), channel_id=1, source_target_pairs={{0,4},{4,8},{8,12},{12,0},{1,5},{5,9},{9,13},{13,1},{2,6},{6,10},{... | collective-permute-start | bytes 1572872 | tf_op jit(solution)/shard_map/ppermute | solution.py:66
  95.0 1.7 %convolution_convert_fusion.1 = bf16[256,1024]{1,0:T(8,128)(2,1)} fusion(bf16[256,1152]{1,0:T(8,128)(2,1)S(1)} %copy-done.3, bf16[1152,1024]{1,0:T(8,128)(2,1)S(1)} %bitcast.16), kind=kOutput, calls=%fused_computation.2 | convolution fusion | flops 604241920 | bytes 3473408 | tf_op jit(solution)/shard_map/dot_general | solution.py:99
  96.7 4.2 %collective-permute-start.5 = (bf16[256,1024]{1,0:T(8,128)(2,1)}, bf16[256,1024]{1,0:T(8,128)(2,1)S(1)}, u32[]{:S(2)}, u32[]{:S(2)}) collective-permute-start(bf16[256,1024]{1,0:T(8,128)(2,1)} %convolution_convert_fusion.1), channel_id=1, source_target_pairs={{0,12},{4,0},{8,4},{12,8},{1,13},{5,1},{9,5},{13,9},{2,14},{6,2},{... | collective-permute-start | bytes 1572872 | tf_op jit(solution)/shard_map/ppermute | solution.py:66
  101.0 0.6 reshape.32
  101.6 0.6 reshape.33
  102.2 2.3 %collective-permute-done.4 = bf16[256,1024]{1,0:T(8,128)(2,1)} collective-permute-done((bf16[256,1024]{1,0:T(8,128)(2,1)}, bf16[256,1024]{1,0:T(8,128)(2,1)}, u32[]{:S(2)}, u32[]{:S(2)}) %collective-permute-start.4) | collective-permute-done | bytes 524320 | tf_op jit(solution)/shard_map/ppermute | solution.py:66
  104.5 2.1 %convert_add_fusion.own_ref = f32[256,1024]{1,0:T(8,128)S(1)} fusion(bf16[256,1024]{1,0:T(8,128)(2,1)} %collective-permute-done.4, bf16[1152,1024]{1,0:T(8,128)(2,1)S(1)} %bitcast.17, bf16[256,4608]{1,0:T(8,128)(2,1)} %param.4, s32[]{:T(128)S(6)} %select_n.24), kind=kOutput, calls=%fused_computation.6 | convolution fusion | flops 604504064 | bytes 4521988 | tf_op jit(solution)/shard_map/dot_general | solution.py:99
  106.6 9.7 %collective-permute-done.6.refs_1_ = bf16[256,1024]{1,0:T(8,128)(2,1)S(1)} collective-permute-done((bf16[256,1024]{1,0:T(8,128)(2,1)}, bf16[256,1024]{1,0:T(8,128)(2,1)S(1)}, u32[]{:S(2)}, u32[]{:S(2)}) %collective-permute-start.6) | collective-permute-done | bytes 524320 | tf_op jit(solution)/shard_map/ppermute | solution.py:66
  116.3 1.0 sum_parts.1
  (13 shorter events, 0.4 us)
Async XLA Ops:
  0.6 16.6 %copy-start = (bf16[256,4608]{1,0:T(8,128)(2,1)S(1)}, bf16[256,4608]{1,0:T(8,128)(2,1)}, u32[]{:S(2)}) copy-start(bf16[256,4608]{1,0:T(8,128)(2,1)} %param.4) | copy-start | bytes 7077892
  2.9 30.5 %all-to-all-start = ((bf16[32,72,128]{2,1,0:T(8,128)(2,1)}), bf16[32,72,128]{2,1,0:T(8,128)(2,1)S(1)}, u32[]{:S(2)}, u32[]{:S(2)}) async-start(bf16[32,72,128]{2,1,0:T(8,128)(2,1)} %reshape.27), calls=%async_computation | async-start | bytes 1179648 | tf_op jit(solution)/shard_map/all_to_all | solution.py:77
  18.4 28.1 %copy-start.1 = (bf16[256,1152]{1,0:T(8,128)(2,1)S(1)}, bf16[256,1152]{1,0:T(8,128)(2,1)}, u32[]{:S(2)}) copy-start(bf16[256,1152]{1,0:T(8,128)(2,1)} %get-tuple-element.35) | copy-start | bytes 1769476
  18.4 17.3 %collective-permute-start = (bf16[256,1152]{1,0:T(8,128)(2,1)}, bf16[256,1152]{1,0:T(8,128)(2,1)S(1)}, u32[]{:S(2)}, u32[]{:S(2)}) collective-permute-start(bf16[256,1152]{1,0:T(8,128)(2,1)} %get-tuple-element.34), channel_id=1, source_target_pairs={{0,4},{4,8},{8,12},{12,0},{1,5},{5,9},{9,13},{13,1},{2,6},{6,10},{... | collective-permute-start | bytes 1769480 | tf_op jit(solution)/shard_map/ppermute | solution.py:66
  35.7 0.8 copy-start.2
  36.5 39.1 %all-to-all-start.1 = ((bf16[64,72,128]{2,1,0:T(8,128)(2,1)}), bf16[64,72,128]{2,1,0:T(8,128)(2,1)S(1)}, u32[]{:S(2)}, u32[]{:S(2)}) async-start(bf16[64,72,128]{2,1,0:T(8,128)(2,1)} %get-tuple-element.18), calls=%async_computation.1 | async-start | bytes 2359296 | tf_op jit(solution)/shard_map/all_to_all | solution.py:90
  46.4 15.8 %collective-permute-start.1 = (bf16[256,1152]{1,0:T(8,128)(2,1)S(1)}, bf16[256,1152]{1,0:T(8,128)(2,1)S(1)}, u32[]{:S(2)}, u32[]{:S(2)}) collective-permute-start(bf16[256,1152]{1,0:T(8,128)(2,1)S(1)} %copy-done.1), channel_id=1, source_target_pairs={{0,8},{4,12},{8,0},{12,4},{1,9},{5,13},{9,1},{13,5},{2,10},{6,14},... | collective-permute-start | bytes 1769480 | tf_op jit(solution)/shard_map/ppermute | solution.py:66
  49.9 25.7 %collective-permute-start.2 = (bf16[256,1152]{1,0:T(8,128)(2,1)S(1)}, bf16[256,1152]{1,0:T(8,128)(2,1)S(1)}, u32[]{:S(2)}, u32[]{:S(2)}) collective-permute-start(bf16[256,1152]{1,0:T(8,128)(2,1)S(1)} %get-tuple-element.33), channel_id=1, source_target_pairs={{0,12},{4,0},{8,4},{12,8},{1,13},{5,1},{9,5},{13,9},{2,14},{6,2},{... | collective-permute-start | bytes 1769480 | tf_op jit(solution)/shard_map/ppermute | solution.py:66
  62.2 0.8 copy-start.4
  76.1 8.5 %collective-permute-start.3 = (bf16[2,288,1024]{2,1,0:T(8,128)(2,1)S(1)}, bf16[2,288,1024]{2,1,0:T(8,128)(2,1)S(1)}, u32[]{:S(2)}, u32[]{:S(2)}) collective-permute-start(bf16[2,288,1024]{2,1,0:T(8,128)(2,1)S(1)} %reshape.30), channel_id=1, source_target_pairs={{0,1},{1,0},{2,3},{3,2},{4,5},{5,4},{6,7},{7,6},{8,9},{9,8},{10,11... | collective-permute-start | bytes 3538952 | tf_op jit(solution)/shard_map/ppermute | solution.py:66
  84.8 1.1 copy-start.5
  87.5 7.5 %copy-start.3 = (bf16[256,1152]{1,0:T(8,128)(2,1)S(1)}, bf16[256,1152]{1,0:T(8,128)(2,1)}, u32[]{:S(2)}) copy-start(bf16[256,1152]{1,0:T(8,128)(2,1)} %copy-done.2) | copy-start | bytes 1769476
  87.5 17.0 %collective-permute-start.4 = (bf16[256,1024]{1,0:T(8,128)(2,1)}, bf16[256,1024]{1,0:T(8,128)(2,1)}, u32[]{:S(2)}, u32[]{:S(2)}) collective-permute-start(bf16[256,1024]{1,0:T(8,128)(2,1)} %convolution_convert_fusion.2), channel_id=1, source_target_pairs={{0,8},{4,12},{8,0},{12,4},{1,9},{5,13},{9,1},{13,5},{2,10},{6,14},... | collective-permute-start | bytes 1572872 | tf_op jit(solution)/shard_map/ppermute | solution.py:66
  92.8 23.6 %collective-permute-start.6 = (bf16[256,1024]{1,0:T(8,128)(2,1)}, bf16[256,1024]{1,0:T(8,128)(2,1)S(1)}, u32[]{:S(2)}, u32[]{:S(2)}) collective-permute-start(bf16[256,1024]{1,0:T(8,128)(2,1)} %convolution_convert_fusion), channel_id=1, source_target_pairs={{0,4},{4,8},{8,12},{12,0},{1,5},{5,9},{9,13},{13,1},{2,6},{6,10},{... | collective-permute-start | bytes 1572872 | tf_op jit(solution)/shard_map/ppermute | solution.py:66
  96.7 19.6 %collective-permute-start.5 = (bf16[256,1024]{1,0:T(8,128)(2,1)}, bf16[256,1024]{1,0:T(8,128)(2,1)S(1)}, u32[]{:S(2)}, u32[]{:S(2)}) collective-permute-start(bf16[256,1024]{1,0:T(8,128)(2,1)} %convolution_convert_fusion.1), channel_id=1, source_target_pairs={{0,12},{4,0},{8,4},{12,8},{1,13},{5,1},{9,5},{13,9},{2,14},{6,2},{... | collective-permute-start | bytes 1572872 | tf_op jit(solution)/shard_map/ppermute | solution.py:66

commit v4 on v3

--- a/solution.py
+++ b/solution.py
@@ -11,7 +11,7 @@
 SIZES = (4, 8, 4, 2, 2)
 REPLICAS = 32
 CHIPS = 64
-ROWS = ("yh", "yl", "z")
+ROWS = ("yh", "z", "yl")
 
 
 def outer_kernel(inner_ref, base_ref, mom_ref, base_out_ref, mom_out_ref, frag_ref):
@@ -42,6 +42,29 @@
         compiler_params=pltpu.CompilerParams(vmem_limit_bytes=8 * 2**20),
         name="outer_step",
     )(got, base, mom)
+
+
+def far_kernel(core_ref, mine_ref, other_ref, act_ref, part_ref, rows_ref):
+    n = mine_ref.shape[1]
+    c = core_ref[0]
+    for h in range(2):
+        rows_ref[pl.ds(pl.multiple_of((2 * h + c) * n, n), n), :] = mine_ref[h]
+        rows_ref[pl.ds(pl.multiple_of((2 * h + 1 - c) * n, n), n), :] = other_ref[h]
+    part_ref[...] = jnp.dot(act_ref[...], rows_ref[...], preferred_element_type=jnp.float32).astype(jnp.bfloat16)
+
+
+def far_product(c, mine, other, act):
+    width = mine.shape[2]
+    whole = pl.BlockSpec(memory_space=pltpu.VMEM)
+    return pl.pallas_call(
+        far_kernel,
+        in_specs=[pl.BlockSpec(memory_space=pltpu.SMEM), whole, whole, whole],
+        out_specs=whole,
+        out_shape=jax.ShapeDtypeStruct((act.shape[0], width), jnp.bfloat16),
+        scratch_shapes=[pltpu.VMEM((act.shape[1], width), jnp.bfloat16)],
+        compiler_params=pltpu.CompilerParams(vmem_limit_bytes=16 * 2**20),
+        name="far_product",
+    )(c.reshape(1), mine, other, act)
 
 
 def sum_kernel(own_ref, *refs):
@@ -88,9 +111,13 @@
     )
     copies, acts[1] = lax.optimization_barrier((copies, acts[1]))
     mine = lax.all_to_all(copies, ROWS, split_axis=0, concat_axis=0, tiled=True)
-    mine, acts[2], acts[-1] = lax.optimization_barrier((mine, acts[2], acts[-1]))
-    mine = mine.reshape(2, REPLICAS * owned, width)
+    base_out, mom_out = base_flat.reshape(owned, width), mom_flat.reshape(owned, width)
+    mine, acts[2], acts[-1], base_out, mom_out = lax.optimization_barrier(
+        (mine, acts[2], acts[-1], base_out, mom_out)
+    )
+    mine = mine.reshape(2, 8, 4, flat, BLK).swapaxes(1, 2).reshape(2, REPLICAS * owned, width)
     other = shift(mine, "c", 1)
+    far = far_product(c, mine, other, acts[2])
     first = jnp.where(c == 0, mine, other)
     second = jnp.where(c == 0, other, mine)
     rows = jnp.stack([first, second], axis=1).reshape(depth, width)
@@ -98,14 +125,12 @@
     def product(a):
         return jnp.dot(a, rows, preferred_element_type=jnp.float32)
 
-    far = product(acts[2]).astype(jnp.bfloat16)
-    far, acts[1], acts[-1] = lax.optimization_barrier((far, acts[1], acts[-1]))
     own = product(columns(0))
     near = [shift(product(acts[by]).astype(jnp.bfloat16), "x", -by) for by in (1, -1)]
     own = own + shift(far, "x", -2).astype(jnp.float32)
     own, *near = lax.optimization_barrier((own, *near))
     keys = sum_parts(own, near)
-    return keys, base_flat.reshape(owned, width), mom_flat.reshape(owned, width)
+    return keys, base_out, mom_out
 
 
 def solution(mesh):

time: 118 us -> 115 us (0.975)
  local copies, waits for them, and re-layouts: 9.42 us -> 7.33 us
    ppermute x7, waiting for transfers between devices: 37.2 us -> 27.8 us  [shift(): return lax.ppermute(v, axis, [(i, (i + by) % n) for i in range(n)])]
    all_to_all x1, waiting for transfers between devices: 0.01 us -> 8.7 us  [body(): mine = lax.all_to_all(copies, ROWS, split_axis=0, concat_axis=0, tiled=True)]
    unnamed x12 -> x6, local copies, waits for them, and re-layouts: 2.5 us -> 0.01 us
    dot_general x4 -> x3, matrix products: 7.16 us -> 6.58 us  [product(): return jnp.dot(a, rows, preferred_element_type=jnp.float32)]
  transfers between devices with their start and end apart: 9 -> 9, of which waited for: 7 -> 9; matrix products, arithmetic and copies ran while one was open for 8% -> 9% of each run, Pallas kernels for 1% -> 1%
where the time goes in v4:
time: 115 us
  starting transfers between devices  49.5 us (43%)
  waiting for transfers between devices  46.6 us (41%)
  local copies, waits for them, and re-layouts  7.33 us (6%)
  matrix products  6.58 us (6%)
  Pallas kernels  3.54 us (3%)
    ppermute x7, waiting for transfers between devices, shift(): return lax.ppermute(v, axis, [(i, (i + by) % n) for i in range(n)])  27.8 us
    ppermute x7, starting transfers between devices, shift(): return lax.ppermute(v, axis, [(i, (i + by) % n) for i in range(n)])  25.3 us
    all_to_all x1, starting transfers between devices, body(): lax.all_to_all(inner_weights.reshape(REPLICAS, flat, BLK), ('yl', 'z'), s...  14.3 us
    all_to_all x1, waiting for transfers between devices, body(): lax.all_to_all(inner_weights.reshape(REPLICAS, flat, BLK), ('yl', 'z'), s...  10.1 us
    all_to_all x1, starting transfers between devices, body(): mine = lax.all_to_all(copies, ROWS, split_axis=0, concat_axis=0, tiled=True)  9.9 us
    all_to_all x1, waiting for transfers between devices, body(): mine = lax.all_to_all(copies, ROWS, split_axis=0, concat_axis=0, tiled=True)  8.7 us
    dot_general x3, matrix products, product(): return jnp.dot(a, rows, preferred_element_type=jnp.float32)  6.58 us
  transfers between devices with their start and end apart: 9, of which 9 were waited for; matrix products, arithmetic and copies ran while one was open for 9% of the time, Pallas kernels for 1%

profile of v4, /device:TPU:1, one launch (start us, length us, event | category | flops | bytes accessed | tf_op | source)
XLA Modules:
  0.0 114.7 jit_solution(427894597782918842)
XLA Ops:
  0.6 2.2 %reshape.33 = bf16[32,72,128]{2,1,0:T(8,128)(2,1)} reshape(bf16[1,288,1024]{2,1,0:T(8,128)(2,1)} %param.7) | data formatting | bytes 1179648 | tf_op jit(solution)/shard_map/reshape | solution.py:101
  2.9 14.3 %all-to-all-start = ((bf16[32,72,128]{2,1,0:T(8,128)(2,1)}), bf16[32,72,128]{2,1,0:T(8,128)(2,1)S(1)}, u32[]{:S(2)}, u32[]{:S(2)}) async-start(bf16[32,72,128]{2,1,0:T(8,128)(2,1)} %reshape.33), calls=%async_computation | async-start | bytes 1179648 | tf_op jit(solution)/shard_map/all_to_all | solution.py:100
  17.2 1.2 %constant_dynamic-slice_fusion = (bf16[256,1152]{1,0:T(8,128)(2,1)}, bf16[256,1152]{1,0:T(8,128)(2,1)}, bf16[256,1152]{1,0:T(8,128)(2,1)S(1)}) fusion(bf16[256,4608]{1,0:T(8,128)(2,1)S(1)} %copy-done.1, s32[]{:T(128)S(6)} %select_n.28, s32[]{:T(128)S(6)} %select_n.26, s32[]{:T(128)S(6)} %select_n.27), kind=kLoop, calls=%fused_computation.9 | loop fusion | bytes 3538956 | tf_op jit(solution)/shard_map/dynamic_slice | solution.py:105
  18.4 3.2 %collective-permute-start = (bf16[256,1152]{1,0:T(8,128)(2,1)}, bf16[256,1152]{1,0:T(8,128)(2,1)}, u32[]{:S(2)}, u32[]{:S(2)}) collective-permute-start(bf16[256,1152]{1,0:T(8,128)(2,1)} %get-tuple-element.32), channel_id=1, source_target_pairs={{0,4},{4,8},{8,12},{12,0},{1,5},{5,9},{9,13},{13,1},{2,6},{6,10},{... | collective-permute-start | bytes 1769480 | tf_op jit(solution)/shard_map/ppermute | solution.py:89
  21.6 0.9 reshape.34.base_ref
  22.5 0.9 reshape.35.mom_ref
  23.4 10.1 %all-to-all-done.inner_ref = bf16[32,72,128]{2,1,0:T(8,128)(2,1)S(1)} async-done(((bf16[32,72,128]{2,1,0:T(8,128)(2,1)}), bf16[32,72,128]{2,1,0:T(8,128)(2,1)S(1)}, u32[]{:S(2)}, u32[]{:S(2)}) %all-to-all-start) | async-done | bytes 589856 | tf_op jit(solution)/shard_map/all_to_all | solution.py:100
  33.4 1.6 %outer_step.1 = (f32[72,128]{1,0:T(8,128)S(1)}, f32[72,128]{1,0:T(8,128)S(1)}, bf16[64,72,128]{2,1,0:T(8,128)(2,1)}) custom-call(bf16[32,72,128]{2,1,0:T(8,128)(2,1)S(1)} %all-to-all-done.inner_ref, f32[72,128]{1,0:T(8,128)S(1)} %reshape.34.base_ref, f32[72,128]{1,0:T(8,128)S(1)} %reshape.35.mom_ref), custom_call_target="tpu_custom_call" | custom-call | tf_op jit(solution)/shard_map/outer_step/pallas_call | solution.py:39
  35.0 0.8 collective-permute-done
  35.8 9.9 %all-to-all-start.1 = ((bf16[64,72,128]{2,1,0:T(8,128)(2,1)}), bf16[64,72,128]{2,1,0:T(8,128)(2,1)S(1)}, u32[]{:S(2)}, u32[]{:S(2)}) async-start(bf16[64,72,128]{2,1,0:T(8,128)(2,1)} %get-tuple-element.17), calls=%async_computation.1 | async-start | bytes 2359296 | tf_op jit(solution)/shard_map/all_to_all | solution.py:113
  45.7 3.2 %collective-permute-start.2 = (bf16[256,1152]{1,0:T(8,128)(2,1)S(1)}, bf16[256,1152]{1,0:T(8,128)(2,1)}, u32[]{:S(2)}, u32[]{:S(2)}) collective-permute-start(bf16[256,1152]{1,0:T(8,128)(2,1)S(1)} %copy-done.2), channel_id=1, source_target_pairs={{0,12},{4,0},{8,4},{12,8},{1,13},{5,1},{9,5},{13,9},{2,14},{6,2},{... | collective-permute-start | bytes 1769480 | tf_op jit(solution)/shard_map/ppermute | solution.py:89
  48.9 2.4 %collective-permute-start.1 = (bf16[256,1152]{1,0:T(8,128)(2,1)S(1)}, bf16[256,1152]{1,0:T(8,128)(2,1)S(1)}, u32[]{:S(2)}, u32[]{:S(2)}) collective-permute-start(bf16[256,1152]{1,0:T(8,128)(2,1)S(1)} %get-tuple-element.33), channel_id=1, source_target_pairs={{0,8},{4,12},{8,0},{12,4},{1,9},{5,13},{9,1},{13,5},{2,10},{6,14},... | collective-permute-start | bytes 1769480 | tf_op jit(solution)/shard_map/ppermute | solution.py:89
  51.4 0.6 reshape.36
  52.0 0.6 reshape.37
  52.6 7.5 %collective-permute-done.2 = bf16[256,1152]{1,0:T(8,128)(2,1)} collective-permute-done((bf16[256,1152]{1,0:T(8,128)(2,1)S(1)}, bf16[256,1152]{1,0:T(8,128)(2,1)}, u32[]{:S(2)}, u32[]{:S(2)}) %collective-permute-start.2) | collective-permute-done | bytes 589856 | tf_op jit(solution)/shard_map/ppermute | solution.py:89
  60.1 4.3 %collective-permute-done.1.act_ref = bf16[256,1152]{1,0:T(8,128)(2,1)S(1)} collective-permute-done((bf16[256,1152]{1,0:T(8,128)(2,1)S(1)}, bf16[256,1152]{1,0:T(8,128)(2,1)S(1)}, u32[]{:S(2)}, u32[]{:S(2)}) %collective-permute-start.1) | collective-permute-done | bytes 589856 | tf_op jit(solution)/shard_map/ppermute | solution.py:89
  64.4 8.7 %all-to-all-done.1 = bf16[64,72,128]{2,1,0:T(8,128)(2,1)S(1)} async-done(((bf16[64,72,128]{2,1,0:T(8,128)(2,1)}), bf16[64,72,128]{2,1,0:T(8,128)(2,1)S(1)}, u32[]{:S(2)}, u32[]{:S(2)}) %all-to-all-start.1) | async-done | bytes 1179680 | tf_op jit(solution)/shard_map/all_to_all | solution.py:113
  73.3 0.5 reshape.39.mine_ref
  73.8 7.7 %collective-permute-start.3 = (bf16[2,288,1024]{2,1,0:T(8,128)(2,1)S(1)}, bf16[2,288,1024]{2,1,0:T(8,128)(2,1)S(1)}, u32[]{:S(2)}, u32[]{:S(2)}) collective-permute-start(bf16[2,288,1024]{2,1,0:T(8,128)(2,1)S(1)} %reshape.39.mine_ref), channel_id=1, source_target_pairs={{0,1},{1,0},{2,3},{3,2},{4,5},{5,4},{6,7},{7,6},{8,9},{9,8},{10,11... | collective-permute-start | bytes 3538952 | tf_op jit(solution)/shard_map/ppermute | solution.py:89
  81.5 2.4 %collective-permute-done.3.other_ref = bf16[2,288,1024]{2,1,0:T(8,128)(2,1)S(1)} collective-permute-done((bf16[2,288,1024]{2,1,0:T(8,128)(2,1)S(1)}, bf16[2,288,1024]{2,1,0:T(8,128)(2,1)S(1)}, u32[]{:S(2)}, u32[]{:S(2)}) %collective-permute-start.3) | collective-permute-done | bytes 1179680 | tf_op jit(solution)/shard_map/ppermute | solution.py:89
  84.2 0.2 pad_maximum_fusion
  84.6 1.0 far_product.1
  85.6 3.4 %collective-permute-start.4 = (bf16[256,1024]{1,0:T(8,128)(2,1)S(1)}, bf16[256,1024]{1,0:T(8,128)(2,1)S(1)}, u32[]{:S(2)}, u32[]{:S(2)}) collective-permute-start(bf16[256,1024]{1,0:T(8,128)(2,1)S(1)} %far_product.1), channel_id=1, source_target_pairs={{0,8},{4,12},{8,0},{12,4},{1,9},{5,13},{9,1},{13,5},{2,10},{6,14},... | collective-permute-start | bytes 1572872 | tf_op jit(solution)/shard_map/ppermute | solution.py:89
  89.1 1.9 %convolution_convert_fusion = bf16[256,1024]{1,0:T(8,128)(2,1)S(1)} fusion(bf16[256,1152]{1,0:T(8,128)(2,1)} %collective-permute-done.2, bf16[1152,1024]{1,0:T(8,128)(2,1)S(1)} %bitcast.17), kind=kOutput, calls=%fused_computation.1 | convolution fusion | flops 604241920 | bytes 3473408 | tf_op jit(solution)/shard_map/dot_general | solution.py:126
  91.0 1.9 %convolution_convert_fusion.1 = bf16[256,1024]{1,0:T(8,128)(2,1)S(1)} fusion(bf16[256,1152]{1,0:T(8,128)(2,1)} %collective-permute-done, bf16[1152,1024]{1,0:T(8,128)(2,1)S(1)} %bitcast.18), kind=kOutput, calls=%fused_computation.2 | convolution fusion | flops 604241920 | bytes 3473408 | tf_op jit(solution)/shard_map/dot_general | solution.py:126
  93.0 2.8 %collective-permute-start.5 = (bf16[256,1024]{1,0:T(8,128)(2,1)S(1)}, bf16[256,1024]{1,0:T(8,128)(2,1)S(1)}, u32[]{:S(2)}, u32[]{:S(2)}) collective-permute-start(bf16[256,1024]{1,0:T(8,128)(2,1)S(1)} %convolution_convert_fusion.1), channel_id=1, source_target_pairs={{0,12},{4,0},{8,4},{12,8},{1,13},{5,1},{9,5},{13,9},{2,14},{6,2},{... | collective-permute-start | bytes 1572872 | tf_op jit(solution)/shard_map/ppermute | solution.py:89
  95.7 2.5 %collective-permute-start.6 = (bf16[256,1024]{1,0:T(8,128)(2,1)S(1)}, bf16[256,1024]{1,0:T(8,128)(2,1)S(1)}, u32[]{:S(2)}, u32[]{:S(2)}) collective-permute-start(bf16[256,1024]{1,0:T(8,128)(2,1)S(1)} %convolution_convert_fusion), channel_id=1, source_target_pairs={{0,4},{4,8},{8,12},{12,0},{1,5},{5,9},{9,13},{13,1},{2,6},{6,10},{... | collective-permute-start | bytes 1572872 | tf_op jit(solution)/shard_map/ppermute | solution.py:89
  98.3 3.9 %collective-permute-done.4 = bf16[256,1024]{1,0:T(8,128)(2,1)S(1)} collective-permute-done((bf16[256,1024]{1,0:T(8,128)(2,1)S(1)}, bf16[256,1024]{1,0:T(8,128)(2,1)S(1)}, u32[]{:S(2)}, u32[]{:S(2)}) %collective-permute-start.4) | collective-permute-done | bytes 524320 | tf_op jit(solution)/shard_map/ppermute | solution.py:89
  102.1 2.7 %convert_add_fusion.own_ref = f32[256,1024]{1,0:T(8,128)S(1)} fusion(bf16[256,1024]{1,0:T(8,128)(2,1)S(1)} %collective-permute-done.4, bf16[1152,1024]{1,0:T(8,128)(2,1)} %bitcast.19, bf16[256,4608]{1,0:T(8,128)(2,1)} %param.4, s32[]{:T(128)S(6)} %select_n.24), kind=kOutput, calls=%fused_computation.6 | convolution fusion | flops 604504064 | bytes 4521988 | tf_op jit(solution)/shard_map/dot_general | solution.py:126
  104.9 7.4 %collective-permute-done.5.refs_0_ = bf16[256,1024]{1,0:T(8,128)(2,1)S(1)} collective-permute-done((bf16[256,1024]{1,0:T(8,128)(2,1)S(1)}, bf16[256,1024]{1,0:T(8,128)(2,1)S(1)}, u32[]{:S(2)}, u32[]{:S(2)}) %collective-permute-start.5) | collective-permute-done | bytes 524320 | tf_op jit(solution)/shard_map/ppermute | solution.py:89
  112.3 1.5 %collective-permute-done.6.refs_1_ = bf16[256,1024]{1,0:T(8,128)(2,1)S(1)} collective-permute-done((bf16[256,1024]{1,0:T(8,128)(2,1)S(1)}, bf16[256,1024]{1,0:T(8,128)(2,1)S(1)}, u32[]{:S(2)}, u32[]{:S(2)}) %collective-permute-start.6) | collective-permute-done | bytes 524320 | tf_op jit(solution)/shard_map/ppermute | solution.py:89
  113.7 1.0 sum_parts.1
  (9 shorter events, 0.5 us)
Async XLA Ops:
  0.6 16.6 %copy-start.1 = (bf16[256,4608]{1,0:T(8,128)(2,1)S(1)}, bf16[256,4608]{1,0:T(8,128)(2,1)}, u32[]{:S(2)}) copy-start(bf16[256,4608]{1,0:T(8,128)(2,1)} %param.4) | copy-start | bytes 7077892
  2.9 30.5 %all-to-all-start = ((bf16[32,72,128]{2,1,0:T(8,128)(2,1)}), bf16[32,72,128]{2,1,0:T(8,128)(2,1)S(1)}, u32[]{:S(2)}, u32[]{:S(2)}) async-start(bf16[32,72,128]{2,1,0:T(8,128)(2,1)} %reshape.33), calls=%async_computation | async-start | bytes 1179648 | tf_op jit(solution)/shard_map/all_to_all | solution.py:100
  18.4 27.3 %copy-start.2 = (bf16[256,1152]{1,0:T(8,128)(2,1)S(1)}, bf16[256,1152]{1,0:T(8,128)(2,1)}, u32[]{:S(2)}) copy-start(bf16[256,1152]{1,0:T(8,128)(2,1)} %get-tuple-element.31) | copy-start | bytes 1769476
  18.4 17.4 %collective-permute-start = (bf16[256,1152]{1,0:T(8,128)(2,1)}, bf16[256,1152]{1,0:T(8,128)(2,1)}, u32[]{:S(2)}, u32[]{:S(2)}) collective-permute-start(bf16[256,1152]{1,0:T(8,128)(2,1)} %get-tuple-element.32), channel_id=1, source_target_pairs={{0,4},{4,8},{8,12},{12,0},{1,5},{5,9},{9,13},{13,1},{2,6},{6,10},{... | collective-permute-start | bytes 1769480 | tf_op jit(solution)/shard_map/ppermute | solution.py:89
  35.8 37.3 %all-to-all-start.1 = ((bf16[64,72,128]{2,1,0:T(8,128)(2,1)}), bf16[64,72,128]{2,1,0:T(8,128)(2,1)S(1)}, u32[]{:S(2)}, u32[]{:S(2)}) async-start(bf16[64,72,128]{2,1,0:T(8,128)(2,1)} %get-tuple-element.17), calls=%async_computation.1 | async-start | bytes 2359296 | tf_op jit(solution)/shard_map/all_to_all | solution.py:113
  45.7 14.4 %collective-permute-start.2 = (bf16[256,1152]{1,0:T(8,128)(2,1)S(1)}, bf16[256,1152]{1,0:T(8,128)(2,1)}, u32[]{:S(2)}, u32[]{:S(2)}) collective-permute-start(bf16[256,1152]{1,0:T(8,128)(2,1)S(1)} %copy-done.2), channel_id=1, source_target_pairs={{0,12},{4,0},{8,4},{12,8},{1,13},{5,1},{9,5},{13,9},{2,14},{6,2},{... | collective-permute-start | bytes 1769480 | tf_op jit(solution)/shard_map/ppermute | solution.py:89
  48.9 15.5 %collective-permute-start.1 = (bf16[256,1152]{1,0:T(8,128)(2,1)S(1)}, bf16[256,1152]{1,0:T(8,128)(2,1)S(1)}, u32[]{:S(2)}, u32[]{:S(2)}) collective-permute-start(bf16[256,1152]{1,0:T(8,128)(2,1)S(1)} %get-tuple-element.33), channel_id=1, source_target_pairs={{0,8},{4,12},{8,0},{12,4},{1,9},{5,13},{9,1},{13,5},{2,10},{6,14},... | collective-permute-start | bytes 1769480 | tf_op jit(solution)/shard_map/ppermute | solution.py:89
  73.8 10.2 %collective-permute-start.3 = (bf16[2,288,1024]{2,1,0:T(8,128)(2,1)S(1)}, bf16[2,288,1024]{2,1,0:T(8,128)(2,1)S(1)}, u32[]{:S(2)}, u32[]{:S(2)}) collective-permute-start(bf16[2,288,1024]{2,1,0:T(8,128)(2,1)S(1)} %reshape.39.mine_ref), channel_id=1, source_target_pairs={{0,1},{1,0},{2,3},{3,2},{4,5},{5,4},{6,7},{7,6},{8,9},{9,8},{10,11... | collective-permute-start | bytes 3538952 | tf_op jit(solution)/shard_map/ppermute | solution.py:89
  84.6 6.4 %copy-start = (bf16[2,2,288,1024]{3,2,1,0:T(8,128)(2,1)}, bf16[2,2,288,1024]{3,2,1,0:T(8,128)(2,1)S(1)}, u32[]{:S(2)}) copy-start(bf16[2,2,288,1024]{3,2,1,0:T(8,128)(2,1)S(1)} %copy.9) | copy-start | bytes 7077892
  85.6 16.5 %collective-permute-start.4 = (bf16[256,1024]{1,0:T(8,128)(2,1)S(1)}, bf16[256,1024]{1,0:T(8,128)(2,1)S(1)}, u32[]{:S(2)}, u32[]{:S(2)}) collective-permute-start(bf16[256,1024]{1,0:T(8,128)(2,1)S(1)} %far_product.1), channel_id=1, source_target_pairs={{0,8},{4,12},{8,0},{12,4},{1,9},{5,13},{9,1},{13,5},{2,10},{6,14},... | collective-permute-start | bytes 1572872 | tf_op jit(solution)/shard_map/ppermute | solution.py:89
  93.0 19.3 %collective-permute-start.5 = (bf16[256,1024]{1,0:T(8,128)(2,1)S(1)}, bf16[256,1024]{1,0:T(8,128)(2,1)S(1)}, u32[]{:S(2)}, u32[]{:S(2)}) collective-permute-start(bf16[256,1024]{1,0:T(8,128)(2,1)S(1)} %convolution_convert_fusion.1), channel_id=1, source_target_pairs={{0,12},{4,0},{8,4},{12,8},{1,13},{5,1},{9,5},{13,9},{2,14},{6,2},{... | collective-permute-start | bytes 1572872 | tf_op jit(solution)/shard_map/ppermute | solution.py:89
  95.7 18.0 %collective-permute-start.6 = (bf16[256,1024]{1,0:T(8,128)(2,1)S(1)}, bf16[256,1024]{1,0:T(8,128)(2,1)S(1)}, u32[]{:S(2)}, u32[]{:S(2)}) collective-permute-start(bf16[256,1024]{1,0:T(8,128)(2,1)S(1)} %convolution_convert_fusion), channel_id=1, source_target_pairs={{0,4},{4,8},{8,12},{12,0},{1,5},{5,9},{9,13},{13,1},{2,6},{6,10},{... | collective-permute-start | bytes 1572872 | tf_op jit(solution)/shard_map/ppermute | solution.py:89

commit v5 on v4

--- a/solution.py
+++ b/solution.py
@@ -62,7 +62,7 @@
         out_specs=whole,
         out_shape=jax.ShapeDtypeStruct((act.shape[0], width), jnp.bfloat16),
         scratch_shapes=[pltpu.VMEM((act.shape[1], width), jnp.bfloat16)],
-        compiler_params=pltpu.CompilerParams(vmem_limit_bytes=16 * 2**20),
+        compiler_params=pltpu.CompilerParams(vmem_limit_bytes=8 * 2**20),
         name="far_product",
     )(c.reshape(1), mine, other, act)
 

time: 115 us -> 115 us (level)
  no operation moved by 1% of the time
where the time goes in v5:
time: 115 us
  starting transfers between devices  49.5 us (43%)
  waiting for transfers between devices  46.6 us (41%)
  local copies, waits for them, and re-layouts  7.33 us (6%)
  matrix products  6.58 us (6%)
  Pallas kernels  3.54 us (3%)
    ppermute x7, waiting for transfers between devices, shift(): return lax.ppermute(v, axis, [(i, (i + by) % n) for i in range(n)])  27.8 us
    ppermute x7, starting transfers between devices, shift(): return lax.ppermute(v, axis, [(i, (i + by) % n) for i in range(n)])  25.3 us
    all_to_all x1, starting transfers between devices, body(): lax.all_to_all(inner_weights.reshape(REPLICAS, flat, BLK), ('yl', 'z'), s...  14.3 us
    all_to_all x1, waiting for transfers between devices, body(): lax.all_to_all(inner_weights.reshape(REPLICAS, flat, BLK), ('yl', 'z'), s...  10.1 us
    all_to_all x1, starting transfers between devices, body(): mine = lax.all_to_all(copies, ROWS, split_axis=0, concat_axis=0, tiled=True)  9.9 us
    all_to_all x1, waiting for transfers between devices, body(): mine = lax.all_to_all(copies, ROWS, split_axis=0, concat_axis=0, tiled=True)  8.7 us
    dot_general x3, matrix products, product(): return jnp.dot(a, rows, preferred_element_type=jnp.float32)  6.58 us
  transfers between devices with their start and end apart: 9, of which 9 were waited for; matrix products, arithmetic and copies ran while one was open for 9% of the time, Pallas kernels for 1%

profile of v5, /device:TPU:1, one launch (start us, length us, event | category | flops | bytes accessed | tf_op | source)
XLA Modules:
  0.0 114.7 jit_solution(427894597782918842)
XLA Ops:
  0.6 2.2 %reshape.33 = bf16[32,72,128]{2,1,0:T(8,128)(2,1)} reshape(bf16[1,288,1024]{2,1,0:T(8,128)(2,1)} %param.7) | data formatting | bytes 1179648 | tf_op jit(solution)/shard_map/reshape | solution.py:101
  2.9 14.3 %all-to-all-start = ((bf16[32,72,128]{2,1,0:T(8,128)(2,1)}), bf16[32,72,128]{2,1,0:T(8,128)(2,1)S(1)}, u32[]{:S(2)}, u32[]{:S(2)}) async-start(bf16[32,72,128]{2,1,0:T(8,128)(2,1)} %reshape.33), calls=%async_computation | async-start | bytes 1179648 | tf_op jit(solution)/shard_map/all_to_all | solution.py:100
  17.2 1.2 %constant_dynamic-slice_fusion = (bf16[256,1152]{1,0:T(8,128)(2,1)}, bf16[256,1152]{1,0:T(8,128)(2,1)}, bf16[256,1152]{1,0:T(8,128)(2,1)S(1)}) fusion(bf16[256,4608]{1,0:T(8,128)(2,1)S(1)} %copy-done.1, s32[]{:T(128)S(6)} %select_n.28, s32[]{:T(128)S(6)} %select_n.26, s32[]{:T(128)S(6)} %select_n.27), kind=kLoop, calls=%fused_computation.9 | loop fusion | bytes 3538956 | tf_op jit(solution)/shard_map/dynamic_slice | solution.py:105
  18.4 3.2 %collective-permute-start = (bf16[256,1152]{1,0:T(8,128)(2,1)}, bf16[256,1152]{1,0:T(8,128)(2,1)}, u32[]{:S(2)}, u32[]{:S(2)}) collective-permute-start(bf16[256,1152]{1,0:T(8,128)(2,1)} %get-tuple-element.32), channel_id=1, source_target_pairs={{0,4},{4,8},{8,12},{12,0},{1,5},{5,9},{9,13},{13,1},{2,6},{6,10},{... | collective-permute-start | bytes 1769480 | tf_op jit(solution)/shard_map/ppermute | solution.py:89
  21.6 0.9 reshape.34.base_ref
  22.5 0.9 reshape.35.mom_ref
  23.4 10.1 %all-to-all-done.inner_ref = bf16[32,72,128]{2,1,0:T(8,128)(2,1)S(1)} async-done(((bf16[32,72,128]{2,1,0:T(8,128)(2,1)}), bf16[32,72,128]{2,1,0:T(8,128)(2,1)S(1)}, u32[]{:S(2)}, u32[]{:S(2)}) %all-to-all-start) | async-done | bytes 589856 | tf_op jit(solution)/shard_map/all_to_all | solution.py:100
  33.4 1.6 %outer_step.1 = (f32[72,128]{1,0:T(8,128)S(1)}, f32[72,128]{1,0:T(8,128)S(1)}, bf16[64,72,128]{2,1,0:T(8,128)(2,1)}) custom-call(bf16[32,72,128]{2,1,0:T(8,128)(2,1)S(1)} %all-to-all-done.inner_ref, f32[72,128]{1,0:T(8,128)S(1)} %reshape.34.base_ref, f32[72,128]{1,0:T(8,128)S(1)} %reshape.35.mom_ref), custom_call_target="tpu_custom_call" | custom-call | tf_op jit(solution)/shard_map/outer_step/pallas_call | solution.py:39
  35.0 0.8 collective-permute-done
  35.8 9.9 %all-to-all-start.1 = ((bf16[64,72,128]{2,1,0:T(8,128)(2,1)}), bf16[64,72,128]{2,1,0:T(8,128)(2,1)S(1)}, u32[]{:S(2)}, u32[]{:S(2)}) async-start(bf16[64,72,128]{2,1,0:T(8,128)(2,1)} %get-tuple-element.17), calls=%async_computation.1 | async-start | bytes 2359296 | tf_op jit(solution)/shard_map/all_to_all | solution.py:113
  45.7 3.2 %collective-permute-start.2 = (bf16[256,1152]{1,0:T(8,128)(2,1)S(1)}, bf16[256,1152]{1,0:T(8,128)(2,1)}, u32[]{:S(2)}, u32[]{:S(2)}) collective-permute-start(bf16[256,1152]{1,0:T(8,128)(2,1)S(1)} %copy-done.2), channel_id=1, source_target_pairs={{0,12},{4,0},{8,4},{12,8},{1,13},{5,1},{9,5},{13,9},{2,14},{6,2},{... | collective-permute-start | bytes 1769480 | tf_op jit(solution)/shard_map/ppermute | solution.py:89
  48.9 2.4 %collective-permute-start.1 = (bf16[256,1152]{1,0:T(8,128)(2,1)S(1)}, bf16[256,1152]{1,0:T(8,128)(2,1)S(1)}, u32[]{:S(2)}, u32[]{:S(2)}) collective-permute-start(bf16[256,1152]{1,0:T(8,128)(2,1)S(1)} %get-tuple-element.33), channel_id=1, source_target_pairs={{0,8},{4,12},{8,0},{12,4},{1,9},{5,13},{9,1},{13,5},{2,10},{6,14},... | collective-permute-start | bytes 1769480 | tf_op jit(solution)/shard_map/ppermute | solution.py:89
  51.4 0.6 reshape.36
  52.0 0.6 reshape.37
  52.6 7.5 %collective-permute-done.2 = bf16[256,1152]{1,0:T(8,128)(2,1)} collective-permute-done((bf16[256,1152]{1,0:T(8,128)(2,1)S(1)}, bf16[256,1152]{1,0:T(8,128)(2,1)}, u32[]{:S(2)}, u32[]{:S(2)}) %collective-permute-start.2) | collective-permute-done | bytes 589856 | tf_op jit(solution)/shard_map/ppermute | solution.py:89
  60.1 4.3 %collective-permute-done.1.act_ref = bf16[256,1152]{1,0:T(8,128)(2,1)S(1)} collective-permute-done((bf16[256,1152]{1,0:T(8,128)(2,1)S(1)}, bf16[256,1152]{1,0:T(8,128)(2,1)S(1)}, u32[]{:S(2)}, u32[]{:S(2)}) %collective-permute-start.1) | collective-permute-done | bytes 589856 | tf_op jit(solution)/shard_map/ppermute | solution.py:89
  64.4 8.7 %all-to-all-done.1 = bf16[64,72,128]{2,1,0:T(8,128)(2,1)S(1)} async-done(((bf16[64,72,128]{2,1,0:T(8,128)(2,1)}), bf16[64,72,128]{2,1,0:T(8,128)(2,1)S(1)}, u32[]{:S(2)}, u32[]{:S(2)}) %all-to-all-start.1) | async-done | bytes 1179680 | tf_op jit(solution)/shard_map/all_to_all | solution.py:113
  73.3 0.5 reshape.39.mine_ref
  73.8 7.7 %collective-permute-start.3 = (bf16[2,288,1024]{2,1,0:T(8,128)(2,1)S(1)}, bf16[2,288,1024]{2,1,0:T(8,128)(2,1)S(1)}, u32[]{:S(2)}, u32[]{:S(2)}) collective-permute-start(bf16[2,288,1024]{2,1,0:T(8,128)(2,1)S(1)} %reshape.39.mine_ref), channel_id=1, source_target_pairs={{0,1},{1,0},{2,3},{3,2},{4,5},{5,4},{6,7},{7,6},{8,9},{9,8},{10,11... | collective-permute-start | bytes 3538952 | tf_op jit(solution)/shard_map/ppermute | solution.py:89
  81.5 2.4 %collective-permute-done.3.other_ref = bf16[2,288,1024]{2,1,0:T(8,128)(2,1)S(1)} collective-permute-done((bf16[2,288,1024]{2,1,0:T(8,128)(2,1)S(1)}, bf16[2,288,1024]{2,1,0:T(8,128)(2,1)S(1)}, u32[]{:S(2)}, u32[]{:S(2)}) %collective-permute-start.3) | collective-permute-done | bytes 1179680 | tf_op jit(solution)/shard_map/ppermute | solution.py:89
  84.2 0.2 pad_maximum_fusion
  84.6 1.0 far_product.1
  85.6 3.4 %collective-permute-start.4 = (bf16[256,1024]{1,0:T(8,128)(2,1)S(1)}, bf16[256,1024]{1,0:T(8,128)(2,1)S(1)}, u32[]{:S(2)}, u32[]{:S(2)}) collective-permute-start(bf16[256,1024]{1,0:T(8,128)(2,1)S(1)} %far_product.1), channel_id=1, source_target_pairs={{0,8},{4,12},{8,0},{12,4},{1,9},{5,13},{9,1},{13,5},{2,10},{6,14},... | collective-permute-start | bytes 1572872 | tf_op jit(solution)/shard_map/ppermute | solution.py:89
  89.1 1.9 %convolution_convert_fusion = bf16[256,1024]{1,0:T(8,128)(2,1)S(1)} fusion(bf16[256,1152]{1,0:T(8,128)(2,1)} %collective-permute-done.2, bf16[1152,1024]{1,0:T(8,128)(2,1)S(1)} %bitcast.17), kind=kOutput, calls=%fused_computation.1 | convolution fusion | flops 604241920 | bytes 3473408 | tf_op jit(solution)/shard_map/dot_general | solution.py:126
  91.0 1.9 %convolution_convert_fusion.1 = bf16[256,1024]{1,0:T(8,128)(2,1)S(1)} fusion(bf16[256,1152]{1,0:T(8,128)(2,1)} %collective-permute-done, bf16[1152,1024]{1,0:T(8,128)(2,1)S(1)} %bitcast.18), kind=kOutput, calls=%fused_computation.2 | convolution fusion | flops 604241920 | bytes 3473408 | tf_op jit(solution)/shard_map/dot_general | solution.py:126
  93.0 2.8 %collective-permute-start.5 = (bf16[256,1024]{1,0:T(8,128)(2,1)S(1)}, bf16[256,1024]{1,0:T(8,128)(2,1)S(1)}, u32[]{:S(2)}, u32[]{:S(2)}) collective-permute-start(bf16[256,1024]{1,0:T(8,128)(2,1)S(1)} %convolution_convert_fusion.1), channel_id=1, source_target_pairs={{0,12},{4,0},{8,4},{12,8},{1,13},{5,1},{9,5},{13,9},{2,14},{6,2},{... | collective-permute-start | bytes 1572872 | tf_op jit(solution)/shard_map/ppermute | solution.py:89
  95.7 2.5 %collective-permute-start.6 = (bf16[256,1024]{1,0:T(8,128)(2,1)S(1)}, bf16[256,1024]{1,0:T(8,128)(2,1)S(1)}, u32[]{:S(2)}, u32[]{:S(2)}) collective-permute-start(bf16[256,1024]{1,0:T(8,128)(2,1)S(1)} %convolution_convert_fusion), channel_id=1, source_target_pairs={{0,4},{4,8},{8,12},{12,0},{1,5},{5,9},{9,13},{13,1},{2,6},{6,10},{... | collective-permute-start | bytes 1572872 | tf_op jit(solution)/shard_map/ppermute | solution.py:89
  98.3 3.9 %collective-permute-done.4 = bf16[256,1024]{1,0:T(8,128)(2,1)S(1)} collective-permute-done((bf16[256,1024]{1,0:T(8,128)(2,1)S(1)}, bf16[256,1024]{1,0:T(8,128)(2,1)S(1)}, u32[]{:S(2)}, u32[]{:S(2)}) %collective-permute-start.4) | collective-permute-done | bytes 524320 | tf_op jit(solution)/shard_map/ppermute | solution.py:89
  102.1 2.7 %convert_add_fusion.own_ref = f32[256,1024]{1,0:T(8,128)S(1)} fusion(bf16[256,1024]{1,0:T(8,128)(2,1)S(1)} %collective-permute-done.4, bf16[1152,1024]{1,0:T(8,128)(2,1)} %bitcast.19, bf16[256,4608]{1,0:T(8,128)(2,1)} %param.4, s32[]{:T(128)S(6)} %select_n.24), kind=kOutput, calls=%fused_computation.6 | convolution fusion | flops 604504064 | bytes 4521988 | tf_op jit(solution)/shard_map/dot_general | solution.py:126
  104.9 7.4 %collective-permute-done.5.refs_0_ = bf16[256,1024]{1,0:T(8,128)(2,1)S(1)} collective-permute-done((bf16[256,1024]{1,0:T(8,128)(2,1)S(1)}, bf16[256,1024]{1,0:T(8,128)(2,1)S(1)}, u32[]{:S(2)}, u32[]{:S(2)}) %collective-permute-start.5) | collective-permute-done | bytes 524320 | tf_op jit(solution)/shard_map/ppermute | solution.py:89
  112.3 1.5 %collective-permute-done.6.refs_1_ = bf16[256,1024]{1,0:T(8,128)(2,1)S(1)} collective-permute-done((bf16[256,1024]{1,0:T(8,128)(2,1)S(1)}, bf16[256,1024]{1,0:T(8,128)(2,1)S(1)}, u32[]{:S(2)}, u32[]{:S(2)}) %collective-permute-start.6) | collective-permute-done | bytes 524320 | tf_op jit(solution)/shard_map/ppermute | solution.py:89
  113.7 1.0 sum_parts.1
  (9 shorter events, 0.5 us)
Async XLA Ops:
  0.6 16.6 %copy-start.1 = (bf16[256,4608]{1,0:T(8,128)(2,1)S(1)}, bf16[256,4608]{1,0:T(8,128)(2,1)}, u32[]{:S(2)}) copy-start(bf16[256,4608]{1,0:T(8,128)(2,1)} %param.4) | copy-start | bytes 7077892
  2.9 30.5 %all-to-all-start = ((bf16[32,72,128]{2,1,0:T(8,128)(2,1)}), bf16[32,72,128]{2,1,0:T(8,128)(2,1)S(1)}, u32[]{:S(2)}, u32[]{:S(2)}) async-start(bf16[32,72,128]{2,1,0:T(8,128)(2,1)} %reshape.33), calls=%async_computation | async-start | bytes 1179648 | tf_op jit(solution)/shard_map/all_to_all | solution.py:100
  18.4 27.3 %copy-start.2 = (bf16[256,1152]{1,0:T(8,128)(2,1)S(1)}, bf16[256,1152]{1,0:T(8,128)(2,1)}, u32[]{:S(2)}) copy-start(bf16[256,1152]{1,0:T(8,128)(2,1)} %get-tuple-element.31) | copy-start | bytes 1769476
  18.4 17.4 %collective-permute-start = (bf16[256,1152]{1,0:T(8,128)(2,1)}, bf16[256,1152]{1,0:T(8,128)(2,1)}, u32[]{:S(2)}, u32[]{:S(2)}) collective-permute-start(bf16[256,1152]{1,0:T(8,128)(2,1)} %get-tuple-element.32), channel_id=1, source_target_pairs={{0,4},{4,8},{8,12},{12,0},{1,5},{5,9},{9,13},{13,1},{2,6},{6,10},{... | collective-permute-start | bytes 1769480 | tf_op jit(solution)/shard_map/ppermute | solution.py:89
  35.8 37.3 %all-to-all-start.1 = ((bf16[64,72,128]{2,1,0:T(8,128)(2,1)}), bf16[64,72,128]{2,1,0:T(8,128)(2,1)S(1)}, u32[]{:S(2)}, u32[]{:S(2)}) async-start(bf16[64,72,128]{2,1,0:T(8,128)(2,1)} %get-tuple-element.17), calls=%async_computation.1 | async-start | bytes 2359296 | tf_op jit(solution)/shard_map/all_to_all | solution.py:113
  45.7 14.4 %collective-permute-start.2 = (bf16[256,1152]{1,0:T(8,128)(2,1)S(1)}, bf16[256,1152]{1,0:T(8,128)(2,1)}, u32[]{:S(2)}, u32[]{:S(2)}) collective-permute-start(bf16[256,1152]{1,0:T(8,128)(2,1)S(1)} %copy-done.2), channel_id=1, source_target_pairs={{0,12},{4,0},{8,4},{12,8},{1,13},{5,1},{9,5},{13,9},{2,14},{6,2},{... | collective-permute-start | bytes 1769480 | tf_op jit(solution)/shard_map/ppermute | solution.py:89
  48.9 15.5 %collective-permute-start.1 = (bf16[256,1152]{1,0:T(8,128)(2,1)S(1)}, bf16[256,1152]{1,0:T(8,128)(2,1)S(1)}, u32[]{:S(2)}, u32[]{:S(2)}) collective-permute-start(bf16[256,1152]{1,0:T(8,128)(2,1)S(1)} %get-tuple-element.33), channel_id=1, source_target_pairs={{0,8},{4,12},{8,0},{12,4},{1,9},{5,13},{9,1},{13,5},{2,10},{6,14},... | collective-permute-start | bytes 1769480 | tf_op jit(solution)/shard_map/ppermute | solution.py:89
  73.8 10.2 %collective-permute-start.3 = (bf16[2,288,1024]{2,1,0:T(8,128)(2,1)S(1)}, bf16[2,288,1024]{2,1,0:T(8,128)(2,1)S(1)}, u32[]{:S(2)}, u32[]{:S(2)}) collective-permute-start(bf16[2,288,1024]{2,1,0:T(8,128)(2,1)S(1)} %reshape.39.mine_ref), channel_id=1, source_target_pairs={{0,1},{1,0},{2,3},{3,2},{4,5},{5,4},{6,7},{7,6},{8,9},{9,8},{10,11... | collective-permute-start | bytes 3538952 | tf_op jit(solution)/shard_map/ppermute | solution.py:89
  84.6 6.4 %copy-start = (bf16[2,2,288,1024]{3,2,1,0:T(8,128)(2,1)}, bf16[2,2,288,1024]{3,2,1,0:T(8,128)(2,1)S(1)}, u32[]{:S(2)}) copy-start(bf16[2,2,288,1024]{3,2,1,0:T(8,128)(2,1)S(1)} %copy.9) | copy-start | bytes 7077892
  85.6 16.5 %collective-permute-start.4 = (bf16[256,1024]{1,0:T(8,128)(2,1)S(1)}, bf16[256,1024]{1,0:T(8,128)(2,1)S(1)}, u32[]{:S(2)}, u32[]{:S(2)}) collective-permute-start(bf16[256,1024]{1,0:T(8,128)(2,1)S(1)} %far_product.1), channel_id=1, source_target_pairs={{0,8},{4,12},{8,0},{12,4},{1,9},{5,13},{9,1},{13,5},{2,10},{6,14},... | collective-permute-start | bytes 1572872 | tf_op jit(solution)/shard_map/ppermute | solution.py:89
  93.0 19.3 %collective-permute-start.5 = (bf16[256,1024]{1,0:T(8,128)(2,1)S(1)}, bf16[256,1024]{1,0:T(8,128)(2,1)S(1)}, u32[]{:S(2)}, u32[]{:S(2)}) collective-permute-start(bf16[256,1024]{1,0:T(8,128)(2,1)S(1)} %convolution_convert_fusion.1), channel_id=1, source_target_pairs={{0,12},{4,0},{8,4},{12,8},{1,13},{5,1},{9,5},{13,9},{2,14},{6,2},{... | collective-permute-start | bytes 1572872 | tf_op jit(solution)/shard_map/ppermute | solution.py:89
  95.7 18.0 %collective-permute-start.6 = (bf16[256,1024]{1,0:T(8,128)(2,1)S(1)}, bf16[256,1024]{1,0:T(8,128)(2,1)S(1)}, u32[]{:S(2)}, u32[]{:S(2)}) collective-permute-start(bf16[256,1024]{1,0:T(8,128)(2,1)S(1)} %convolution_convert_fusion), channel_id=1, source_target_pairs={{0,4},{4,8},{8,12},{12,0},{1,5},{5,9},{9,13},{13,1},{2,6},{6,10},{... | collective-permute-start | bytes 1572872 | tf_op jit(solution)/shard_map/ppermute | solution.py:89

commit v6 on v4

--- a/solution.py
+++ b/solution.py
@@ -97,9 +97,8 @@
     flat = owned * width // BLK
     depth = activations.shape[1] // nx
 
-    got = lax.all_to_all(
-        inner_weights.reshape(REPLICAS, flat, BLK), ("yl", "z"), split_axis=0, concat_axis=0, tiled=True
-    )
+    sent = inner_weights.reshape(4, 8, flat, BLK).swapaxes(0, 1).reshape(REPLICAS, flat, BLK)
+    got = lax.all_to_all(sent, ("z", "yl"), split_axis=0, concat_axis=0, tiled=True)
 
     def columns(by):
         return lax.dynamic_slice_in_dim(activations, lax.rem(x + (by + nx), nx) * depth, depth, axis=1)

time: 115 us -> 117 us (1.017)
  waiting for transfers between devices: 46.6 us -> 47.9 us
    reshape x1 -> x2, local copies, waits for them, and re-layouts: 2.24 us -> 2.37 us  [body(): inner_weights.reshape(4, 8, flat, BLK).swapaxes(0, 1)]
  transfers between devices with their start and end apart: 9 -> 9, of which waited for: 9 -> 9; matrix products, arithmetic and copies ran while one was open for 9% -> 8% of each run, Pallas kernels for 1% -> 1%
where the time goes in v6:
time: 117 us; the launch traced here: 116 us
  starting transfers between devices  49.5 us (42%)
  waiting for transfers between devices  47.9 us (41%)
  local copies, waits for them, and re-layouts  8.28 us (7%)
  matrix products  5.51 us (5%)
  Pallas kernels  3.57 us (3%)
    ppermute x7, waiting for transfers between devices, shift(): return lax.ppermute(v, axis, [(i, (i + by) % n) for i in range(n)])  28.9 us
    ppermute x7, starting transfers between devices, shift(): return lax.ppermute(v, axis, [(i, (i + by) % n) for i in range(n)])  25.4 us
    all_to_all x1, starting transfers between devices, body(): lax.all_to_all(sent, ('z', 'yl'), split_axis=0, concat_axis=0, tiled=True)  14.3 us
    all_to_all x1, waiting for transfers between devices, body(): lax.all_to_all(sent, ('z', 'yl'), split_axis=0, concat_axis=0, tiled=True)  10.2 us
    all_to_all x1, starting transfers between devices, body(): mine = lax.all_to_all(copies, ROWS, split_axis=0, concat_axis=0, tiled=True)  9.83 us
    all_to_all x1, waiting for transfers between devices, body(): mine = lax.all_to_all(copies, ROWS, split_axis=0, concat_axis=0, tiled=True)  8.7 us
    dot_general x3, matrix products, product(): return jnp.dot(a, rows, preferred_element_type=jnp.float32)  5.51 us
    reshape x2, local copies, waits for them, and re-layouts, body(): inner_weights.reshape(4, 8, flat, BLK).swapaxes(0, 1)  2.37 us
  transfers between devices with their start and end apart: 9, of which 9 were waited for; matrix products, arithmetic and copies ran while one was open for 8% of the time, Pallas kernels for 1%

profile of v6, /device:TPU:1, one launch (start us, length us, event | category | flops | bytes accessed | tf_op | source)
XLA Modules:
  0.0 116.0 jit_solution(2434531576930500621)
XLA Ops:
  0.6 1.5 %reshape.36 = bf16[4,8,72,128]{3,2,1,0:T(8,128)(2,1)S(1)} reshape(bf16[1,288,1024]{2,1,0:T(8,128)(2,1)} %param.7) | data formatting | bytes 1179648 | tf_op jit(solution)/shard_map/reshape | solution.py:100
  2.1 0.9 copy.9
  3.0 14.3 %all-to-all-start = ((bf16[32,72,128]{2,1,0:T(8,128)(2,1)}), bf16[32,72,128]{2,1,0:T(8,128)(2,1)S(1)}, u32[]{:S(2)}, u32[]{:S(2)}) async-start(bf16[32,72,128]{2,1,0:T(8,128)(2,1)} %bitcast.1), calls=%async_computation | async-start | bytes 1179648 | tf_op jit(solution)/shard_map/all_to_all | solution.py:101
  17.4 1.2 %constant_dynamic-slice_fusion = (bf16[256,1152]{1,0:T(8,128)(2,1)}, bf16[256,1152]{1,0:T(8,128)(2,1)}, bf16[256,1152]{1,0:T(8,128)(2,1)S(1)}) fusion(bf16[256,4608]{1,0:T(8,128)(2,1)S(1)} %copy-done.1, s32[]{:T(128)S(6)} %select_n.28, s32[]{:T(128)S(6)} %select_n.26, s32[]{:T(128)S(6)} %select_n.27), kind=kLoop, calls=%fused_computation.9 | loop fusion | bytes 3538956 | tf_op jit(solution)/shard_map/dynamic_slice | solution.py:104
  18.5 3.2 %collective-permute-start = (bf16[256,1152]{1,0:T(8,128)(2,1)}, bf16[256,1152]{1,0:T(8,128)(2,1)S(1)}, u32[]{:S(2)}, u32[]{:S(2)}) collective-permute-start(bf16[256,1152]{1,0:T(8,128)(2,1)} %get-tuple-element.32), channel_id=1, source_target_pairs={{0,4},{4,8},{8,12},{12,0},{1,5},{5,9},{9,13},{13,1},{2,6},{6,10},{... | collective-permute-start | bytes 1769480 | tf_op jit(solution)/shard_map/ppermute | solution.py:89
  21.8 0.9 reshape.38.base_ref
  22.6 0.9 reshape.39.mom_ref
  23.5 10.2 %all-to-all-done.inner_ref = bf16[32,72,128]{2,1,0:T(8,128)(2,1)S(1)} async-done(((bf16[32,72,128]{2,1,0:T(8,128)(2,1)}), bf16[32,72,128]{2,1,0:T(8,128)(2,1)S(1)}, u32[]{:S(2)}, u32[]{:S(2)}) %all-to-all-start) | async-done | bytes 589856 | tf_op jit(solution)/shard_map/all_to_all | solution.py:101
  33.7 1.6 %outer_step.1 = (f32[72,128]{1,0:T(8,128)S(1)}, f32[72,128]{1,0:T(8,128)S(1)}, bf16[64,72,128]{2,1,0:T(8,128)(2,1)}) custom-call(bf16[32,72,128]{2,1,0:T(8,128)(2,1)S(1)} %all-to-all-done.inner_ref, f32[72,128]{1,0:T(8,128)S(1)} %reshape.38.base_ref, f32[72,128]{1,0:T(8,128)S(1)} %reshape.39.mom_ref), custom_call_target="tpu_custom_call" | custom-call | tf_op jit(solution)/shard_map/outer_step/pallas_call | solution.py:39
  35.3 0.6 collective-permute-done
  35.8 0.8 copy-done.3
  36.7 9.8 %all-to-all-start.1 = ((bf16[64,72,128]{2,1,0:T(8,128)(2,1)}), bf16[64,72,128]{2,1,0:T(8,128)(2,1)S(1)}, u32[]{:S(2)}, u32[]{:S(2)}) async-start(bf16[64,72,128]{2,1,0:T(8,128)(2,1)} %get-tuple-element.17), calls=%async_computation.1 | async-start | bytes 2359296 | tf_op jit(solution)/shard_map/all_to_all | solution.py:112
  46.5 3.2 %collective-permute-start.2 = (bf16[256,1152]{1,0:T(8,128)(2,1)S(1)}, bf16[256,1152]{1,0:T(8,128)(2,1)}, u32[]{:S(2)}, u32[]{:S(2)}) collective-permute-start(bf16[256,1152]{1,0:T(8,128)(2,1)S(1)} %copy-done.2), channel_id=1, source_target_pairs={{0,12},{4,0},{8,4},{12,8},{1,13},{5,1},{9,5},{13,9},{2,14},{6,2},{... | collective-permute-start | bytes 1769480 | tf_op jit(solution)/shard_map/ppermute | solution.py:89
  49.7 2.4 %collective-permute-start.1 = (bf16[256,1152]{1,0:T(8,128)(2,1)S(1)}, bf16[256,1152]{1,0:T(8,128)(2,1)S(1)}, u32[]{:S(2)}, u32[]{:S(2)}) collective-permute-start(bf16[256,1152]{1,0:T(8,128)(2,1)S(1)} %get-tuple-element.33), channel_id=1, source_target_pairs={{0,8},{4,12},{8,0},{12,4},{1,9},{5,13},{9,1},{13,5},{2,10},{6,14},... | collective-permute-start | bytes 1769480 | tf_op jit(solution)/shard_map/ppermute | solution.py:89
  52.1 0.6 reshape.40
  52.8 0.6 reshape.41
  53.4 7.5 %collective-permute-done.2 = bf16[256,1152]{1,0:T(8,128)(2,1)} collective-permute-done((bf16[256,1152]{1,0:T(8,128)(2,1)S(1)}, bf16[256,1152]{1,0:T(8,128)(2,1)}, u32[]{:S(2)}, u32[]{:S(2)}) %collective-permute-start.2) | collective-permute-done | bytes 589856 | tf_op jit(solution)/shard_map/ppermute | solution.py:89
  60.9 4.3 %collective-permute-done.1.act_ref = bf16[256,1152]{1,0:T(8,128)(2,1)S(1)} collective-permute-done((bf16[256,1152]{1,0:T(8,128)(2,1)S(1)}, bf16[256,1152]{1,0:T(8,128)(2,1)S(1)}, u32[]{:S(2)}, u32[]{:S(2)}) %collective-permute-start.1) | collective-permute-done | bytes 589856 | tf_op jit(solution)/shard_map/ppermute | solution.py:89
  65.2 8.7 %all-to-all-done.1 = bf16[64,72,128]{2,1,0:T(8,128)(2,1)S(1)} async-done(((bf16[64,72,128]{2,1,0:T(8,128)(2,1)}), bf16[64,72,128]{2,1,0:T(8,128)(2,1)S(1)}, u32[]{:S(2)}, u32[]{:S(2)}) %all-to-all-start.1) | async-done | bytes 1179680 | tf_op jit(solution)/shard_map/all_to_all | solution.py:112
  74.6 7.7 %collective-permute-start.3 = (bf16[2,288,1024]{2,1,0:T(8,128)(2,1)S(1)}, bf16[2,288,1024]{2,1,0:T(8,128)(2,1)S(1)}, u32[]{:S(2)}, u32[]{:S(2)}) collective-permute-start(bf16[2,288,1024]{2,1,0:T(8,128)(2,1)S(1)} %reshape.43.mine_ref), channel_id=1, source_target_pairs={{0,1},{1,0},{2,3},{3,2},{4,5},{5,4},{6,7},{7,6},{8,9},{9,8},{10,11... | collective-permute-start | bytes 3538952 | tf_op jit(solution)/shard_map/ppermute | solution.py:89
  82.3 2.4 %collective-permute-done.3.other_ref = bf16[2,288,1024]{2,1,0:T(8,128)(2,1)S(1)} collective-permute-done((bf16[2,288,1024]{2,1,0:T(8,128)(2,1)S(1)}, bf16[2,288,1024]{2,1,0:T(8,128)(2,1)S(1)}, u32[]{:S(2)}, u32[]{:S(2)}) %collective-permute-start.3) | collective-permute-done | bytes 1179680 | tf_op jit(solution)/shard_map/ppermute | solution.py:89
  85.4 1.0 far_product.1
  86.4 3.6 %collective-permute-start.4 = (bf16[256,1024]{1,0:T(8,128)(2,1)S(1)}, bf16[256,1024]{1,0:T(8,128)(2,1)S(1)}, u32[]{:S(2)}, u32[]{:S(2)}) collective-permute-start(bf16[256,1024]{1,0:T(8,128)(2,1)S(1)} %far_product.1), channel_id=1, source_target_pairs={{0,8},{4,12},{8,0},{12,4},{1,9},{5,13},{9,1},{13,5},{2,10},{6,14},... | collective-permute-start | bytes 1572872 | tf_op jit(solution)/shard_map/ppermute | solution.py:89
  90.0 1.9 %convolution_convert_fusion = bf16[256,1024]{1,0:T(8,128)(2,1)S(1)} fusion(bf16[256,1152]{1,0:T(8,128)(2,1)} %collective-permute-done.2, bf16[1152,1024]{1,0:T(8,128)(2,1)S(1)} %bitcast.20), kind=kOutput, calls=%fused_computation.1 | convolution fusion | flops 604241920 | bytes 3473408 | tf_op jit(solution)/shard_map/dot_general | solution.py:125
  92.0 0.9 convolution_convert_fusion.1
  92.8 2.8 %collective-permute-start.5 = (bf16[256,1024]{1,0:T(8,128)(2,1)S(1)}, bf16[256,1024]{1,0:T(8,128)(2,1)S(1)}, u32[]{:S(2)}, u32[]{:S(2)}) collective-permute-start(bf16[256,1024]{1,0:T(8,128)(2,1)S(1)} %convolution_convert_fusion.1), channel_id=1, source_target_pairs={{0,12},{4,0},{8,4},{12,8},{1,13},{5,1},{9,5},{13,9},{2,14},{6,2},{... | collective-permute-start | bytes 1572872 | tf_op jit(solution)/shard_map/ppermute | solution.py:89
  95.6 2.5 %collective-permute-start.6 = (bf16[256,1024]{1,0:T(8,128)(2,1)S(1)}, bf16[256,1024]{1,0:T(8,128)(2,1)S(1)}, u32[]{:S(2)}, u32[]{:S(2)}) collective-permute-start(bf16[256,1024]{1,0:T(8,128)(2,1)S(1)} %convolution_convert_fusion), channel_id=1, source_target_pairs={{0,4},{4,8},{8,12},{12,0},{1,5},{5,9},{9,13},{13,1},{2,6},{6,10},{... | collective-permute-start | bytes 1572872 | tf_op jit(solution)/shard_map/ppermute | solution.py:89
  98.1 5.0 %collective-permute-done.4 = bf16[256,1024]{1,0:T(8,128)(2,1)S(1)} collective-permute-done((bf16[256,1024]{1,0:T(8,128)(2,1)S(1)}, bf16[256,1024]{1,0:T(8,128)(2,1)S(1)}, u32[]{:S(2)}, u32[]{:S(2)}) %collective-permute-start.4) | collective-permute-done | bytes 524320 | tf_op jit(solution)/shard_map/ppermute | solution.py:89
  103.1 2.7 %convert_add_fusion.own_ref = f32[256,1024]{1,0:T(8,128)S(1)} fusion(bf16[256,1024]{1,0:T(8,128)(2,1)S(1)} %collective-permute-done.4, bf16[1152,1024]{1,0:T(8,128)(2,1)} %bitcast.22, bf16[256,4608]{1,0:T(8,128)(2,1)} %param.4, s32[]{:T(128)S(6)} %select_n.24), kind=kOutput, calls=%fused_computation.6 | convolution fusion | flops 604504064 | bytes 4521988 | tf_op jit(solution)/shard_map/dot_general | solution.py:125
  105.8 7.4 %collective-permute-done.5.refs_0_ = bf16[256,1024]{1,0:T(8,128)(2,1)S(1)} collective-permute-done((bf16[256,1024]{1,0:T(8,128)(2,1)S(1)}, bf16[256,1024]{1,0:T(8,128)(2,1)S(1)}, u32[]{:S(2)}, u32[]{:S(2)}) %collective-permute-start.5) | collective-permute-done | bytes 524320 | tf_op jit(solution)/shard_map/ppermute | solution.py:89
  113.2 1.8 %collective-permute-done.6.refs_1_ = bf16[256,1024]{1,0:T(8,128)(2,1)S(1)} collective-permute-done((bf16[256,1024]{1,0:T(8,128)(2,1)S(1)}, bf16[256,1024]{1,0:T(8,128)(2,1)S(1)}, u32[]{:S(2)}, u32[]{:S(2)}) %collective-permute-start.6) | collective-permute-done | bytes 524320 | tf_op jit(solution)/shard_map/ppermute | solution.py:89
  115.0 1.0 sum_parts.1
  (14 shorter events, 1.3 us)
Async XLA Ops:
  0.6 16.7 %copy-start.1 = (bf16[256,4608]{1,0:T(8,128)(2,1)S(1)}, bf16[256,4608]{1,0:T(8,128)(2,1)}, u32[]{:S(2)}) copy-start(bf16[256,4608]{1,0:T(8,128)(2,1)} %param.4) | copy-start | bytes 7077892
  3.0 30.7 %all-to-all-start = ((bf16[32,72,128]{2,1,0:T(8,128)(2,1)}), bf16[32,72,128]{2,1,0:T(8,128)(2,1)S(1)}, u32[]{:S(2)}, u32[]{:S(2)}) async-start(bf16[32,72,128]{2,1,0:T(8,128)(2,1)} %bitcast.1), calls=%async_computation | async-start | bytes 1179648 | tf_op jit(solution)/shard_map/all_to_all | solution.py:101
  18.5 28.0 %copy-start.2 = (bf16[256,1152]{1,0:T(8,128)(2,1)S(1)}, bf16[256,1152]{1,0:T(8,128)(2,1)}, u32[]{:S(2)}) copy-start(bf16[256,1152]{1,0:T(8,128)(2,1)} %get-tuple-element.31) | copy-start | bytes 1769476
  18.5 17.3 %collective-permute-start = (bf16[256,1152]{1,0:T(8,128)(2,1)}, bf16[256,1152]{1,0:T(8,128)(2,1)S(1)}, u32[]{:S(2)}, u32[]{:S(2)}) collective-permute-start(bf16[256,1152]{1,0:T(8,128)(2,1)} %get-tuple-element.32), channel_id=1, source_target_pairs={{0,4},{4,8},{8,12},{12,0},{1,5},{5,9},{9,13},{13,1},{2,6},{6,10},{... | collective-permute-start | bytes 1769480 | tf_op jit(solution)/shard_map/ppermute | solution.py:89
  35.8 0.8 copy-start.3
  36.7 37.2 %all-to-all-start.1 = ((bf16[64,72,128]{2,1,0:T(8,128)(2,1)}), bf16[64,72,128]{2,1,0:T(8,128)(2,1)S(1)}, u32[]{:S(2)}, u32[]{:S(2)}) async-start(bf16[64,72,128]{2,1,0:T(8,128)(2,1)} %get-tuple-element.17), calls=%async_computation.1 | async-start | bytes 2359296 | tf_op jit(solution)/shard_map/all_to_all | solution.py:112
  46.5 14.4 %collective-permute-start.2 = (bf16[256,1152]{1,0:T(8,128)(2,1)S(1)}, bf16[256,1152]{1,0:T(8,128)(2,1)}, u32[]{:S(2)}, u32[]{:S(2)}) collective-permute-start(bf16[256,1152]{1,0:T(8,128)(2,1)S(1)} %copy-done.2), channel_id=1, source_target_pairs={{0,12},{4,0},{8,4},{12,8},{1,13},{5,1},{9,5},{13,9},{2,14},{6,2},{... | collective-permute-start | bytes 1769480 | tf_op jit(solution)/shard_map/ppermute | solution.py:89
  49.7 15.5 %collective-permute-start.1 = (bf16[256,1152]{1,0:T(8,128)(2,1)S(1)}, bf16[256,1152]{1,0:T(8,128)(2,1)S(1)}, u32[]{:S(2)}, u32[]{:S(2)}) collective-permute-start(bf16[256,1152]{1,0:T(8,128)(2,1)S(1)} %get-tuple-element.33), channel_id=1, source_target_pairs={{0,8},{4,12},{8,0},{12,4},{1,9},{5,13},{9,1},{13,5},{2,10},{6,14},... | collective-permute-start | bytes 1769480 | tf_op jit(solution)/shard_map/ppermute | solution.py:89
  74.6 10.2 %collective-permute-start.3 = (bf16[2,288,1024]{2,1,0:T(8,128)(2,1)S(1)}, bf16[2,288,1024]{2,1,0:T(8,128)(2,1)S(1)}, u32[]{:S(2)}, u32[]{:S(2)}) collective-permute-start(bf16[2,288,1024]{2,1,0:T(8,128)(2,1)S(1)} %reshape.43.mine_ref), channel_id=1, source_target_pairs={{0,1},{1,0},{2,3},{3,2},{4,5},{5,4},{6,7},{7,6},{8,9},{9,8},{10,11... | collective-permute-start | bytes 3538952 | tf_op jit(solution)/shard_map/ppermute | solution.py:89
  85.4 6.6 %copy-start = (bf16[2,2,288,1024]{3,2,1,0:T(8,128)(2,1)}, bf16[2,2,288,1024]{3,2,1,0:T(8,128)(2,1)S(1)}, u32[]{:S(2)}) copy-start(bf16[2,2,288,1024]{3,2,1,0:T(8,128)(2,1)S(1)} %copy.11) | copy-start | bytes 7077892
  86.4 5.5 %copy-start.4 = (bf16[256,1152]{1,0:T(8,128)(2,1)S(1)}, bf16[256,1152]{1,0:T(8,128)(2,1)}, u32[]{:S(2)}) copy-start(bf16[256,1152]{1,0:T(8,128)(2,1)} %copy-done.3) | copy-start | bytes 1769476
  86.4 16.7 %collective-permute-start.4 = (bf16[256,1024]{1,0:T(8,128)(2,1)S(1)}, bf16[256,1024]{1,0:T(8,128)(2,1)S(1)}, u32[]{:S(2)}, u32[]{:S(2)}) collective-permute-start(bf16[256,1024]{1,0:T(8,128)(2,1)S(1)} %far_product.1), channel_id=1, source_target_pairs={{0,8},{4,12},{8,0},{12,4},{1,9},{5,13},{9,1},{13,5},{2,10},{6,14},... | collective-permute-start | bytes 1572872 | tf_op jit(solution)/shard_map/ppermute | solution.py:89
  92.8 20.4 %collective-permute-start.5 = (bf16[256,1024]{1,0:T(8,128)(2,1)S(1)}, bf16[256,1024]{1,0:T(8,128)(2,1)S(1)}, u32[]{:S(2)}, u32[]{:S(2)}) collective-permute-start(bf16[256,1024]{1,0:T(8,128)(2,1)S(1)} %convolution_convert_fusion.1), channel_id=1, source_target_pairs={{0,12},{4,0},{8,4},{12,8},{1,13},{5,1},{9,5},{13,9},{2,14},{6,2},{... | collective-permute-start | bytes 1572872 | tf_op jit(solution)/shard_map/ppermute | solution.py:89
  95.6 19.4 %collective-permute-start.6 = (bf16[256,1024]{1,0:T(8,128)(2,1)S(1)}, bf16[256,1024]{1,0:T(8,128)(2,1)S(1)}, u32[]{:S(2)}, u32[]{:S(2)}) collective-permute-start(bf16[256,1024]{1,0:T(8,128)(2,1)S(1)} %convolution_convert_fusion), channel_id=1, source_target_pairs={{0,4},{4,8},{8,12},{12,0},{1,5},{5,9},{9,13},{13,1},{2,6},{6,10},{... | collective-permute-start | bytes 1572872 | tf_op jit(solution)/shard_map/ppermute | solution.py:89
